TPU v7x, 32 devices: a whole 2x2x4 slice. The times are simulated.
32 devices in a mesh: blk: 8 (over z, y), rep: 4 (over x, core).
Axes of the slice: x: 2, y: 2, z: 4, core: 2. Of those that a mesh axis runs over, the one named last changes fastest.
Arguments:
- features: bfloat16 [4096, 256], P('blk'), may hold values from -6 to 6
- weight: bfloat16 [256, 256], replicated, may hold values from -0.375 to 0.375
- cotangent: bfloat16 [4096, 256], P(('blk', 'rep')), may hold values from -6 to 6
- tile_values: bfloat16 [8, 8, 12, 128, 128], P('blk', 'rep'), may hold values from -0.15625 to 0.15625
- tile_rows: int32 [8, 8, 12], P('blk', 'rep'), may hold values from 0 to 3, as said below
- tile_cols: int32 [8, 8, 12], P('blk', 'rep'), may hold values from 0 to 3
- tile_count: int32 [8, 8], P('blk', 'rep'), may hold values from 1 to 12, as said below
Outputs:
- activations: bfloat16 [4096, 256], P(('blk', 'rep'))
- weight_grad: float32 [256, 256], replicated
- feature_grad: bfloat16 [4096, 256], P(('blk', 'rep'))
Inputs may be any that keep to these rules, and one draw needn't show every extreme that they name: Among the live slots of one list the pairs (tile_rows, tile_cols) are distinct. `tile_count`: the list of a block with itself (offset 0) always has 12 live slots.
All inputs are finite; a program needn't handle non-finite values.
Results may differ from a plain program's by a relative error of at most 0.024.
Values may be sent and summed in bfloat16 or wider, within the bound.
A program may use at most 64 MiB of HBM per device.

v0:
```python
import math

import jax
import jax.numpy as jnp
from jax import lax
from jax.sharding import PartitionSpec as P


def from_behind(shard, axis, by):
    size = lax.axis_size(axis)
    return lax.ppermute(shard, axis, [(i, (i + by) % size) for i in range(size)])


def dense_block(tiles, rows, cols, count, rows_blk):
    row_tiles = rows_blk // 128
    live = jnp.arange(tiles.shape[0], dtype=jnp.int32) < count
    targets = jnp.arange(row_tiles, dtype=jnp.int32)
    col_hot = ((cols[:, None] == targets[None, :]) & live[:, None]).astype(jnp.bfloat16)
    row_hot = (rows[:, None] == targets[None, :]).astype(jnp.bfloat16)
    placed = jnp.einsum("sc,sij->sicj", col_hot, tiles, preferred_element_type=jnp.float32).astype(
        jnp.bfloat16
    )
    placed = placed.reshape(tiles.shape[0], 128, rows_blk)
    whole = jnp.einsum("sr,sik->rik", row_hot, placed, preferred_element_type=jnp.float32).astype(
        jnp.bfloat16
    )
    return whole.reshape(rows_blk, rows_blk)


def forward_padded(tiles, rows, cols, count, block):
    matrix = dense_block(tiles, rows, cols, count, block.shape[0])
    return jnp.dot(matrix, block, preferred_element_type=jnp.float32)


def backward_padded(tiles, rows, cols, count, grads):
    matrix = dense_block(tiles, rows, cols, count, grads.shape[0])
    return lax.dot_general(
        matrix, grads, (((0,), (0,)), ((), ())), preferred_element_type=jnp.float32
    )


def silu_parts(z_value, cot_rows):
    sigma = jax.nn.sigmoid(z_value)
    output = (z_value * sigma).astype(jnp.bfloat16)
    slope = (cot_rows.astype(jnp.float32) * sigma * (1.0 + z_value * (1.0 - sigma))).astype(
        jnp.bfloat16
    )
    return (output, slope)


def per_device(features, weight, cotangent, tile_values, tile_rows, tile_cols, tile_count):
    rows_blk, width = features.shape
    sections = tile_count.shape[1]
    replicas = lax.axis_size("rep")
    rep_index = lax.axis_index("rep")
    bit_count = replicas.bit_length() - 1
    nodes = rows_blk * lax.axis_size("blk")
    block = features
    for bit in range(bit_count):
        moved = from_behind(block, "blk", -(sections << bit))
        block = jnp.where(rep_index >> bit & 1 == 1, moved, block)
    partial_value = jnp.zeros((rows_blk, width), jnp.float32)
    for section in range(sections):
        partial_value = partial_value + forward_padded(
            tile_values[0, section],
            tile_rows[0, section],
            tile_cols[0, section],
            tile_count[0, section],
            block,
        )
        if section + 1 < sections:
            block = from_behind(block, "blk", -1)
    agg = lax.psum_scatter(partial_value, "rep", scatter_dimension=0, tiled=True).astype(
        jnp.bfloat16
    )
    z_value = jnp.dot(agg, weight, preferred_element_type=jnp.float32)
    activations, dz_value = silu_parts(z_value, cotangent)
    weight_term = jnp.dot(agg.T, dz_value, preferred_element_type=jnp.float32)
    dy_rows = jnp.dot(dz_value, weight.T, preferred_element_type=jnp.float32).astype(jnp.bfloat16)
    dy_block = lax.all_gather(dy_rows, "rep", axis=0, tiled=True)
    weight_grad = lax.psum(weight_term, ("blk", "rep")) / math.sqrt(nodes)
    carried = jnp.zeros((rows_blk, width), jnp.float32)
    for section in reversed(range(sections)):
        carried = carried + backward_padded(
            tile_values[0, section],
            tile_rows[0, section],
            tile_cols[0, section],
            tile_count[0, section],
            dy_block,
        )
        if section > 0:
            carried = from_behind(carried, "blk", 1)
    for bit in range(bit_count):
        moved = from_behind(carried.astype(jnp.bfloat16), "blk", sections << bit).astype(
            carried.dtype
        )
        carried = jnp.where(rep_index >> bit & 1 == 1, moved, carried)
    feature_grad = lax.psum_scatter(
        carried.astype(jnp.bfloat16), "rep", scatter_dimension=0, tiled=True
    )
    return (activations, weight_grad, feature_grad)


def solution(mesh):
    return jax.shard_map(
        per_device,
        mesh=mesh,
        in_specs=(
            P("blk", None),
            P(),
            P(("blk", "rep"), None),
            P("blk", "rep", None, None, None),
            P("blk", "rep", None),
            P("blk", "rep", None),
            P("blk", "rep"),
        ),
        out_specs=(P(("blk", "rep"), None), P(), P(("blk", "rep"), None)),
        check_vma=False,
    )
```

profile of v0, /device:TPU:0, one launch (start us, length us, event | category | flops | bytes accessed | tf_op | source)
XLA Modules:
  0.0 258.6 jit_solution(69789411451242753)
XLA Ops:
  7.2 5.1 %collective-permute-start = (bf16[512,256]{1,0:T(8,128)(2,1)}, bf16[512,256]{1,0:T(8,128)(2,1)}, u32[]{:S(2)}, u32[]{:S(2)}) collective-permute-start(bf16[512,256]{1,0:T(8,128)(2,1)} %param.7), channel_id=1, source_target_pairs={{0,24},{4,28},{8,0},{12,4},{16,8},{20,12},{24,16},{28,20},{1,25},{... | collective-permute-start | bytes 786440 | tf_op jit(solution)/shard_map/ppermute | solution.py:11
  12.3 1.2 bitcast_convert_fusion.1
  13.6 0.3 copy.15
  13.9 0.6 fusion.15
  14.5 0.6 iota_compare_fusion.5
  15.1 0.7 iota_compare_fusion.4
  15.9 1.5 multiply_convert_fusion
  17.4 3.5 %copy.16 = bf16[12,128,512]{2,0,1:T(8,128)(2,1)S(1)} copy(bf16[12,128,512]{1,2,0:T(8,128)(2,1)} %bitcast.42) | data formatting | bytes 3145728 | tf_op jit(solution)/shard_map/reshape | solution.py:23
  20.9 0.4 convolution_convert_fusion
  21.8 0.6 copy-done.1
  22.4 1.5 multiply_convert_fusion.1
  24.0 3.5 %copy.13 = bf16[12,128,512]{2,0,1:T(8,128)(2,1)S(1)} copy(bf16[12,128,512]{1,2,0:T(8,128)(2,1)} %bitcast.43) | data formatting | bytes 3145728 | tf_op jit(solution)/shard_map/reshape | solution.py:23
  27.5 8.0 %collective-permute-done.1 = bf16[512,256]{1,0:T(8,128)(2,1)S(1)} collective-permute-done((bf16[512,256]{1,0:T(8,128)(2,1)S(1)}, bf16[512,256]{1,0:T(8,128)(2,1)S(1)}, u32[]{:S(2)}, u32[]{:S(2)}) %collective-permute-start.1) | collective-permute-done | bytes 262176 | tf_op jit(solution)/shard_map/ppermute | solution.py:11
  35.5 3.6 %collective-permute-start.2 = (bf16[512,256]{1,0:T(8,128)(2,1)S(1)}, bf16[512,256]{1,0:T(8,128)(2,1)S(1)}, u32[]{:S(2)}, u32[]{:S(2)}) collective-permute-start(bf16[512,256]{1,0:T(8,128)(2,1)S(1)} %broadcast_select_fusion.1), channel_id=1, source_target_pairs={{0,28},{4,0},{8,4},{12,8},{16,12},{20,16},{24,20},{28,24},{1,29},{... | collective-permute-start | bytes 786440 | tf_op jit(solution)/shard_map/ppermute | solution.py:11
  39.2 0.4 convolution_convert_fusion.1
  39.7 4.9 %collective-permute-done.2 = bf16[512,256]{1,0:T(8,128)(2,1)S(1)} collective-permute-done((bf16[512,256]{1,0:T(8,128)(2,1)S(1)}, bf16[512,256]{1,0:T(8,128)(2,1)S(1)}, u32[]{:S(2)}, u32[]{:S(2)}) %collective-permute-start.2) | collective-permute-done | bytes 262176 | tf_op jit(solution)/shard_map/ppermute | solution.py:11
  44.6 0.3 fusion.16
  44.9 1.1 convolution_add_fusion.1
  46.1 23.6 %reduce-scatter.3.cloned.1.call-done = f32[128,256]{1,0:T(8,128)} async-done(((f32[512,256]{1,0:T(8,128)}), f32[128,256]{1,0:T(8,128)}) %reduce-scatter.3.cloned.1.call-update) | async-done | bytes 131088 | tf_op jit(solution)/shard_map/reduce_scatter | solution.py:73
  69.7 1.7 multiply_convert_fusion.3
  71.6 5.9 %all_gather.3 = bf16[512,256]{1,0:T(8,128)(2,1)S(1)} all-gather(bf16[128,256]{1,0:T(8,128)(2,1)S(1)} %convolution_convert_fusion.2), channel_id=1, replica_groups=mesh['blk'=8,'rep'=4] {'rep'}, dimensions={0}, use_global_device_ids=true | all-gather | bytes 327680 | tf_op jit(solution)/shard_map/all_gather | solution.py:80
  77.6 0.3 fusion.17
  77.9 1.5 collective-permute-start.3
  79.5 15.4 %collective-permute-done.3 = f32[512,256]{1,0:T(8,128)S(1)} collective-permute-done((f32[512,256]{1,0:T(8,128)S(1)}, f32[512,256]{1,0:T(8,128)S(1)}, u32[]{:S(2)}, u32[]{:S(2)}) %collective-permute-start.3) | collective-permute-done | bytes 524320 | tf_op jit(solution)/shard_map/ppermute | solution.py:11
  94.8 0.3 convolution_add_fusion
  95.2 9.5 %collective-permute-done.4 = bf16[512,256]{1,0:T(8,128)(2,1)S(1)} collective-permute-done((bf16[512,256]{1,0:T(8,128)(2,1)S(1)}, bf16[512,256]{1,0:T(8,128)(2,1)S(1)}, u32[]{:S(2)}, u32[]{:S(2)}) %collective-permute-start.4) | collective-permute-done | bytes 262176 | tf_op jit(solution)/shard_map/ppermute | solution.py:11
  104.9 0.9 fusion.1
  106.0 10.8 %collective-permute-done.5 = bf16[512,256]{1,0:T(8,128)(2,1)S(1)} collective-permute-done((bf16[512,256]{1,0:T(8,128)(2,1)S(1)}, bf16[512,256]{1,0:T(8,128)(2,1)S(1)}, u32[]{:S(2)}, u32[]{:S(2)}) %collective-permute-start.5) | collective-permute-done | bytes 262176 | tf_op jit(solution)/shard_map/ppermute | solution.py:11
  116.8 0.8 select_convert_fusion
  117.6 112.2 %all-reduce.2.cloned.1.call-done = f32[256,256]{1,0:T(8,128)} async-done(((f32[256,256]{1,0:T(8,128)}), f32[256,256]{1,0:T(8,128)}) %all-reduce.2.cloned.1.call-update) | async-done | bytes 262160 | tf_op jit(solution)/shard_map/psum | solution.py:81
  229.8 1.7 broadcast_multiply_fusion
  231.5 20.6 %reduce-scatter.5.cloned.1.call-done = bf16[128,256]{1,0:T(8,128)(2,1)} async-done(((bf16[512,256]{1,0:T(8,128)(2,1)}), bf16[128,256]{1,0:T(8,128)(2,1)}) %reduce-scatter.5.cloned.1.call-update) | async-done | bytes 65552 | tf_op jit(solution)/shard_map/reduce_scatter | solution.py:98
  (33 shorter events, 1.3 us)
Async XLA Ops:
  7.2 62.5 %copy-start = (bf16[256,256]{1,0:T(8,128)(2,1)S(1)}, bf16[256,256]{1,0:T(8,128)(2,1)}, u32[]{:S(2)}) copy-start(bf16[256,256]{1,0:T(8,128)(2,1)} %param.8) | copy-start | bytes 393220
  7.2 6.7 %copy-start.3 = (s32[1,2,12]{2,1,0:T(2,128)S(1)}, s32[1,2,12]{2,1,0:T(2,128)}, u32[]{:S(2)}) copy-start(s32[1,2,12]{2,1,0:T(2,128)} %param.12) | copy-start | bytes 292
  7.2 6.7 %copy-start.2 = (s32[1,2]{1,0:T(1,128)S(1)}, s32[1,2]{1,0:T(1,128)}, u32[]{:S(2)}) copy-start(s32[1,2]{1,0:T(1,128)} %param.13) | copy-start | bytes 28
  7.2 62.5 %reduce-scatter.3.cloned.1.call-start = ((), (), s32[]{:S(2)}) async-start(), calls=%async_computation.2 | async-start | bytes 655360 | tf_op jit(solution)/shard_map/reduce_scatter | solution.py:73
  7.2 14.5 %collective-permute-start = (bf16[512,256]{1,0:T(8,128)(2,1)}, bf16[512,256]{1,0:T(8,128)(2,1)}, u32[]{:S(2)}, u32[]{:S(2)}) collective-permute-start(bf16[512,256]{1,0:T(8,128)(2,1)} %param.7), channel_id=1, source_target_pairs={{0,24},{4,28},{8,0},{12,4},{16,8},{20,12},{24,16},{28,20},{1,25},{... | collective-permute-start | bytes 786440 | tf_op jit(solution)/shard_map/ppermute | solution.py:11
  17.4 3.5 %copy-start.4 = (s32[1,2,12]{2,1,0:T(2,128)S(1)}, s32[1,2,12]{2,1,0:T(2,128)}, u32[]{:S(2)}) copy-start(s32[1,2,12]{2,1,0:T(2,128)} %param.11) | copy-start | bytes 292
  21.4 1.0 copy-start.1
  22.4 13.1 %collective-permute-start.1 = (bf16[512,256]{1,0:T(8,128)(2,1)S(1)}, bf16[512,256]{1,0:T(8,128)(2,1)S(1)}, u32[]{:S(2)}, u32[]{:S(2)}) collective-permute-start(bf16[512,256]{1,0:T(8,128)(2,1)S(1)} %broadcast_select_fusion), channel_id=1, source_target_pairs={{0,16},{4,20},{8,24},{12,28},{16,0},{20,4},{24,8},{28,12},{1,17},{... | collective-permute-start | bytes 786440 | tf_op jit(solution)/shard_map/ppermute | solution.py:11
  35.5 9.1 %collective-permute-start.2 = (bf16[512,256]{1,0:T(8,128)(2,1)S(1)}, bf16[512,256]{1,0:T(8,128)(2,1)S(1)}, u32[]{:S(2)}, u32[]{:S(2)}) collective-permute-start(bf16[512,256]{1,0:T(8,128)(2,1)S(1)} %broadcast_select_fusion.1), channel_id=1, source_target_pairs={{0,28},{4,0},{8,4},{12,8},{16,12},{20,16},{24,20},{28,24},{1,29},{... | collective-permute-start | bytes 786440 | tf_op jit(solution)/shard_map/ppermute | solution.py:11
  44.6 26.8 %copy-start.6 = (bf16[128,256]{1,0:T(8,128)(2,1)S(1)}, bf16[128,256]{1,0:T(8,128)(2,1)}, u32[]{:S(2)}) copy-start(bf16[128,256]{1,0:T(8,128)(2,1)} %param.9) | copy-start | bytes 196612
  46.0 183.8 %all-reduce.2.cloned.1.call-start = ((), (), s32[]{:S(2)}) async-start(), calls=%async_computation.3 | async-start | bytes 524288 | tf_op jit(solution)/shard_map/psum | solution.py:81
  71.6 33.3 %copy-start.5 = (f32[128,256]{1,0:T(8,128)S(1)}, f32[128,256]{1,0:T(8,128)}, u32[]{:S(2)}) copy-start(f32[128,256]{1,0:T(8,128)} %reduce-scatter.3.cloned.1.call-done) | copy-start | bytes 393220
  77.9 16.9 %collective-permute-start.3 = (f32[512,256]{1,0:T(8,128)S(1)}, f32[512,256]{1,0:T(8,128)S(1)}, u32[]{:S(2)}, u32[]{:S(2)}) collective-permute-start(f32[512,256]{1,0:T(8,128)S(1)} %fusion.17), channel_id=1, source_target_pairs={{0,4},{4,8},{8,12},{12,16},{16,20},{20,24},{24,28},{28,0},{1,5},{5... | collective-permute-start | bytes 1572872 | tf_op jit(solution)/shard_map/ppermute | solution.py:11
  95.2 9.6 %collective-permute-start.4 = (bf16[512,256]{1,0:T(8,128)(2,1)S(1)}, bf16[512,256]{1,0:T(8,128)(2,1)S(1)}, u32[]{:S(2)}, u32[]{:S(2)}) collective-permute-start(bf16[512,256]{1,0:T(8,128)(2,1)S(1)} %convolution_add_fusion), channel_id=1, source_target_pairs={{0,8},{4,12},{8,16},{12,20},{16,24},{20,28},{24,0},{28,4},{1,9},{5... | collective-permute-start | bytes 786440 | tf_op jit(solution)/shard_map/ppermute | solution.py:11
  104.9 11.9 %collective-permute-start.5 = (bf16[512,256]{1,0:T(8,128)(2,1)S(1)}, bf16[512,256]{1,0:T(8,128)(2,1)S(1)}, u32[]{:S(2)}, u32[]{:S(2)}) collective-permute-start(bf16[512,256]{1,0:T(8,128)(2,1)S(1)} %fusion), channel_id=1, source_target_pairs={{0,16},{4,20},{8,24},{12,28},{16,0},{20,4},{24,8},{28,12},{1,17},{... | collective-permute-start | bytes 786440 | tf_op jit(solution)/shard_map/ppermute | solution.py:11
  105.9 146.2 %reduce-scatter.5.cloned.1.call-start = ((), (), s32[]{:S(2)}) async-start(), calls=%async_computation.4 | async-start | bytes 327680 | tf_op jit(solution)/shard_map/reduce_scatter | solution.py:98
Sparse Core Ops, SparseCore 0:
  46.1 23.5 reduce-scatter.2
  106.0 123.7 all-reduce.1
  233.0 19.0 reduce-scatter.4
where the time goes:
time: 259 us
  waiting for transfers between devices  205 us (79%)
  between operations  14 us (5%)
  starting transfers between devices  10.6 us (4%)
  local copies, waits for them, and re-layouts  8.91 us (3%)
  other arithmetic  8.23 us (3%)
  blocking collectives  5.92 us (2%)
  matrix products  5.79 us (2%)
    psum x1, waiting for transfers between devices, per_device(): weight_grad = lax.psum(weight_term, ('blk', 'rep')) / math.sqrt(nodes)  112 us
    ppermute x6, waiting for transfers between devices, from_behind(): lax.ppermute(shard, axis, [(i, (i + by) % size) for i in range(size)])  48.7 us
    reduce_scatter x1, waiting for transfers between devices, per_device(): lax.psum_scatter(partial_value, 'rep', scatter_dimension=0, tiled=True)  23.6 us
    reduce_scatter x1, waiting for transfers between devices, per_device(): lax.psum_scatter(carried.astype(jnp.bfloat16), 'rep', scatter_dimension=0...  20.6 us
    ppermute x6, starting transfers between devices, from_behind(): lax.ppermute(shard, axis, [(i, (i + by) % size) for i in range(size)])  10.5 us
    reshape x2, local copies, waits for them, and re-layouts, dense_block(): placed = placed.reshape(tiles.shape[0], 128, rows_blk)  7.02 us
    all_gather x1, blocking collectives, per_device(): dy_block = lax.all_gather(dy_rows, 'rep', axis=0, tiled=True)  5.92 us
  transfers between devices with their start and end apart: 9, of which 8 were waited for; matrix products, arithmetic and copies ran while one was open for 7% of the time, Pallas kernels for 0%

commit v1 on v0

v1 whole, which is shorter than its diff:
```python
import functools
import math

import jax
import jax.numpy as jnp
from jax import lax
from jax.experimental import pallas as pl
from jax.experimental.pallas import tpu as pltpu
from jax.sharding import PartitionSpec as P

MESH = pl.DeviceIdType.MESH
TILE = 128
UNROLL = 8


def repeat(count, body, first=0):
    if count - first <= UNROLL:
        for index in range(first, count):
            body(index)
    else:

        def step(index, carry):
            body(index)
            return carry

        lax.fori_loop(first, count, step, 0)


def kernel(dims, *refs):
    blocks, replicas, sections, rows_blk, width, slots, own_rows, w_rows, w_chunk, nodes = dims
    (feat, weight, cot, tiles, trows, tcols, tcount) = refs[:7]
    (act, wgrad, fgrad) = refs[7:10]
    (fbuf, amat, amat_t, pbuf, rbuf, dzfull, agg_t, aggs, gbuf, gslots, wpart, wslots, wcol) = refs[10:23]
    (f_send, f_recv, p_send, p_recv, z_send, z_recv, a_send, a_recv) = refs[23:31]
    (g_send, g_recv, w_send, w_recv, c_send, c_recv, r_send, r_recv) = refs[31:]
    b = lax.axis_index("blk")
    r = lax.axis_index("rep")
    row_tiles = rows_blk // TILE
    whole_weight = w_chunk > 0

    def blk_at(offset):
        return lax.rem(b + offset + 2 * blocks, blocks)

    def remote(src, dst, send, recv, to):
        return pltpu.make_async_remote_copy(
            src_ref=src, dst_ref=dst, send_sem=send, recv_sem=recv, device_id=to, device_id_type=MESH
        )

    barrier = pltpu.get_barrier_semaphore()

    def greet(to):
        pl.semaphore_signal(barrier, inc=1, device_id=to, device_id_type=MESH)

    repeat(replicas, lambda d: greet((b, lax.rem(r + d, replicas))), 1)
    repeat(blocks, lambda d: greet((blk_at(d), r)), 1)

    def greet_grad(o):
        source = o // sections

        @pl.when(jnp.logical_or(o != 0, r != 0))
        def _():
            greet((blk_at(-o), source))

    repeat(blocks, greet_grad)
    own = jnp.where(r == 0, 1, 0)
    pl.semaphore_wait(barrier, replicas - 1 + blocks - 1 + sections * replicas - own)

    def feature_copy(s):
        return remote(
            feat, fbuf.at[s], f_send.at[s], f_recv.at[s], (blk_at(-(sections * r + s)), r)
        )

    for s in range(sections):
        if s == 0:

            @pl.when(r != 0)
            def _():
                feature_copy(0).start()

            @pl.when(r == 0)
            def _():
                fbuf[0] = feat[...]
        else:
            feature_copy(s).start()

    for s in range(sections):
        count = tcount[0, s]
        place = [
            jnp.where(t < count, trows[0, s, t] * row_tiles + tcols[0, s, t], -1)
            for t in range(slots)
        ]
        for i in range(row_tiles):
            for j in range(row_tiles):
                slot = jnp.int32(0)
                for t in range(slots):
                    slot = jnp.where(place[t] == i * row_tiles + j, t + 1, slot)
                tile = tiles[0, s, jnp.maximum(slot - 1, 0)]
                tile = jnp.where(slot > 0, tile, jnp.zeros_like(tile))
                at_row = pl.ds(i * TILE, TILE)
                at_col = pl.ds(s * rows_blk + j * TILE, TILE)
                amat[at_row, at_col] = tile
                amat_t[at_col, at_row] = tile.T

    for s in range(sections):
        if s == 0:

            @pl.when(r != 0)
            def _():
                feature_copy(0).wait()
        else:
            feature_copy(s).wait()

    def partial_rows(k):
        total = jnp.zeros((own_rows, width), jnp.float32)
        at_row = pl.ds(pl.multiple_of(k * own_rows, own_rows), own_rows)
        for s in range(sections):
            total = total + jnp.dot(
                amat[at_row, s * rows_blk : (s + 1) * rows_blk],
                fbuf[s],
                preferred_element_type=jnp.float32,
            )
        return total

    def partial_copy(d):
        return remote(
            pbuf.at[d - 1],
            rbuf.at[d - 1],
            p_send.at[d - 1],
            p_recv.at[d - 1],
            (b, lax.rem(r + d, replicas)),
        )

    def send_partial(d):
        pbuf[d - 1] = partial_rows(lax.rem(r + d, replicas)).astype(pbuf.dtype)
        partial_copy(d).start()

    repeat(replicas, send_partial, 1)
    total = partial_rows(r)
    repeat(replicas, lambda d: partial_copy(d).wait(), 1)
    for d in range(1, replicas):
        total = total + rbuf[d - 1].astype(jnp.float32)
    agg = total.astype(jnp.bfloat16)

    z_value = jnp.dot(agg, weight[...], preferred_element_type=jnp.float32)
    sigma = jax.nn.sigmoid(z_value)
    dz = (cot[...].astype(jnp.float32) * sigma * (1.0 + z_value * (1.0 - sigma))).astype(jnp.bfloat16)
    mine = pl.ds(pl.multiple_of(r * own_rows, own_rows), own_rows)
    dzfull[mine, :] = dz

    def dz_copy(d):
        return remote(
            dzfull.at[mine],
            dzfull.at[mine],
            z_send.at[d - 1],
            z_recv.at[d - 1],
            (b, lax.rem(r + d, replicas)),
        )

    def dz_arrival(d):
        source = lax.rem(r + replicas - d, replicas)
        at_row = pl.ds(pl.multiple_of(source * own_rows, own_rows), own_rows)
        return remote(
            dzfull.at[at_row], dzfull.at[at_row], z_send.at[d - 1], z_recv.at[d - 1], (b, source)
        )

    repeat(replicas, lambda d: dz_copy(d).start(), 1)
    agg_t[...] = agg.T

    def agg_copy(d):
        peer = lax.rem(r + d, replicas)
        at_row = pl.ds(pl.multiple_of(peer * w_rows, w_rows), w_rows)
        return remote(agg_t.at[at_row], aggs.at[d], a_send.at[d - 1], a_recv.at[d - 1], (b, peer))

    repeat(replicas, lambda d: agg_copy(d).start(), 1)
    aggs[0] = agg_t[pl.ds(pl.multiple_of(r * w_rows, w_rows), w_rows), :]
    act[...] = (z_value * sigma).astype(jnp.bfloat16)

    repeat(replicas, lambda d: dz_arrival(d).wait_recv(), 1)
    dy = lax.dot_general(
        dzfull[...], weight[...], (((1,), (1,)), ((), ())), preferred_element_type=jnp.float32
    ).astype(jnp.bfloat16)

    def grad_copy(s, k):
        o = sections * r + s
        return remote(
            gbuf.at[s, k], gslots.at[o], g_send.at[s, k], g_recv.at[o], (blk_at(o), k)
        )

    def send_grad(s, k):
        at_row = pl.ds(s * rows_blk + k * own_rows, own_rows)
        gbuf[s, k] = jnp.dot(amat_t[at_row, :], dy, preferred_element_type=jnp.float32).astype(
            gbuf.dtype
        )
        if s == 0 and k == 0:

            @pl.when(r != 0)
            def _():
                grad_copy(s, k).start()

            @pl.when(r == 0)
            def _():
                gslots[0] = gbuf[0, 0]
        else:
            grad_copy(s, k).start()

    def weight_rows():
        repeat(replicas, lambda d: agg_copy(d).wait_recv(), 1)
        acc = jnp.zeros((w_rows, width), jnp.float32)
        for d in range(replicas):
            source = lax.rem(r + replicas - d, replicas)
            at_row = pl.ds(pl.multiple_of(source * own_rows, own_rows), own_rows)
            acc = acc + jnp.dot(aggs[d], dzfull[at_row, :], preferred_element_type=jnp.float32)
        return acc * (1.0 / math.sqrt(nodes))

    def chunk_of(at):
        return pl.ds(pl.multiple_of(at * w_chunk, w_chunk), w_chunk)

    def w_copy(d):
        return remote(
            wpart.at[chunk_of(blk_at(d))], wslots.at[d - 1], w_send.at[d - 1], w_recv.at[d - 1], (blk_at(d), r)
        )

    def c_copy(d):
        return remote(
            wcol.at[chunk_of(b)], wcol.at[chunk_of(b)], c_send.at[d - 1], c_recv.at[d - 1], (blk_at(d), r)
        )

    def c_arrival(d):
        at_row = chunk_of(blk_at(-d))
        return remote(wcol.at[at_row], wcol.at[at_row], c_send.at[d - 1], c_recv.at[d - 1], (blk_at(-d), r))

    def r_copy(d):
        at_row = pl.ds(pl.multiple_of(r * w_rows, w_rows), w_rows)
        return remote(
            wcol, wgrad.at[at_row], r_send.at[d - 1], r_recv.at[d - 1], (b, lax.rem(r + d, replicas))
        )

    def r_arrival(d):
        source = lax.rem(r + replicas - d, replicas)
        at_row = pl.ds(pl.multiple_of(source * w_rows, w_rows), w_rows)
        return remote(wcol, wgrad.at[at_row], r_send.at[d - 1], r_recv.at[d - 1], (b, source))

    if whole_weight:
        wpart[...] = weight_rows()
        repeat(blocks, lambda d: w_copy(d).start(), 1)
    else:
        wgrad[...] = weight_rows()

    for s in reversed(range(sections)):
        for k in range(replicas):
            send_grad(s, k)

    if whole_weight:
        repeat(blocks, lambda d: w_copy(d).wait_recv(), 1)
        chunk = wpart[chunk_of(b), :]
        for d in range(1, blocks):
            chunk = chunk + wslots[d - 1]
        wcol[chunk_of(b), :] = chunk
        repeat(blocks, lambda d: c_copy(d).start(), 1)
        repeat(blocks, lambda d: c_arrival(d).wait_recv(), 1)
        repeat(replicas, lambda d: r_copy(d).start(), 1)
        wgrad[pl.ds(pl.multiple_of(r * w_rows, w_rows), w_rows), :] = wcol[...]

    def grad_arrival(o):
        copy = remote(
            gslots.at[o], gslots.at[o], g_send.at[0, 0], g_recv.at[o], (blk_at(-o), o // sections)
        )

        @pl.when(jnp.logical_or(o != 0, r != 0))
        def _():
            copy.wait_recv()

    repeat(blocks, grad_arrival)
    summed = gslots[0].astype(jnp.float32)
    for o in range(1, blocks):
        summed = summed + gslots[o].astype(jnp.float32)
    fgrad[...] = summed.astype(jnp.bfloat16)

    repeat(replicas, lambda d: dz_copy(d).wait_send(), 1)
    repeat(replicas, lambda d: agg_copy(d).wait_send(), 1)
    for s in range(sections):
        for k in range(replicas):
            if s == 0 and k == 0:

                @pl.when(r != 0)
                def _():
                    grad_copy(s, k).wait_send()
            else:
                grad_copy(s, k).wait_send()
    if whole_weight:
        repeat(blocks, lambda d: w_copy(d).wait_send(), 1)
        repeat(blocks, lambda d: c_copy(d).wait_send(), 1)
        repeat(replicas, lambda d: r_arrival(d).wait_recv(), 1)
        repeat(replicas, lambda d: r_copy(d).wait_send(), 1)


def per_device(features, weight, cotangent, tile_values, tile_rows, tile_cols, tile_count):
    rows_blk, width = features.shape
    sections, slots = tile_rows.shape[1:]
    replicas = lax.axis_size("rep")
    blocks = lax.axis_size("blk")
    nodes = rows_blk * blocks
    own_rows = rows_blk // replicas
    w_rows = width // replicas
    w_chunk = w_rows // blocks if w_rows % (8 * blocks) == 0 else 0
    dims = (blocks, replicas, sections, rows_blk, width, slots, own_rows, w_rows, w_chunk, nodes)
    bf16, f32 = jnp.bfloat16, jnp.float32
    vmem = pl.BlockSpec(memory_space=pltpu.VMEM)
    smem = pl.BlockSpec(memory_space=pltpu.SMEM)
    dma = pltpu.SemaphoreType.DMA
    others = max(replicas - 1, 1)
    act, wgrad, fgrad = pl.pallas_call(
        functools.partial(kernel, dims),
        out_shape=(
            jax.ShapeDtypeStruct((own_rows, width), bf16),
            jax.ShapeDtypeStruct((width if w_chunk else w_rows, width), f32),
            jax.ShapeDtypeStruct((own_rows, width), bf16),
        ),
        in_specs=[vmem] * 4 + [smem] * 3,
        out_specs=(vmem, vmem, vmem),
        scratch_shapes=[
            pltpu.VMEM((sections, rows_blk, width), bf16),
            pltpu.VMEM((rows_blk, sections * rows_blk), bf16),
            pltpu.VMEM((sections * rows_blk, rows_blk), bf16),
            pltpu.VMEM((others, own_rows, width), bf16),
            pltpu.VMEM((others, own_rows, width), bf16),
            pltpu.VMEM((rows_blk, width), bf16),
            pltpu.VMEM((width, own_rows), bf16),
            pltpu.VMEM((replicas, w_rows, own_rows), bf16),
            pltpu.VMEM((sections, replicas, own_rows, width), bf16),
            pltpu.VMEM((blocks, own_rows, width), bf16),
            pltpu.VMEM((w_rows, width), f32),
            pltpu.VMEM((blocks, max(w_chunk, 8), width), f32),
            pltpu.VMEM((w_rows, width), f32),
            dma((sections,)),
            dma((sections,)),
            dma((others,)),
            dma((others,)),
            dma((others,)),
            dma((others,)),
            dma((others,)),
            dma((others,)),
            dma((sections, replicas)),
            dma((blocks,)),
            dma((blocks,)),
            dma((blocks,)),
            dma((blocks,)),
            dma((blocks,)),
            dma((others,)),
            dma((others,)),
        ],
        compiler_params=pltpu.CompilerParams(
            collective_id=0, has_side_effects=True, vmem_limit_bytes=24 * 1024 * 1024
        ),
        name="graph_layer",
    )(features, weight, cotangent, tile_values, tile_rows, tile_cols, tile_count)
    if not w_chunk:
        wgrad = lax.all_gather(lax.psum(wgrad, "blk"), "rep", axis=0, tiled=True)
    return (act, wgrad, fgrad)


def solution(mesh):
    return jax.shard_map(
        per_device,
        mesh=mesh,
        in_specs=(
            P("blk", None),
            P(),
            P(("blk", "rep"), None),
            P("blk", "rep", None, None, None),
            P("blk", "rep", None),
            P("blk", "rep", None),
            P("blk", "rep"),
        ),
        out_specs=(P(("blk", "rep"), None), P(), P(("blk", "rep"), None)),
        check_vma=False,
    )
```

time: 259 us -> 67.1 us (0.26)
  waiting for transfers between devices: 205 us -> 0 us
  Pallas kernels: 0 us -> 58.3 us
  between operations: 14 us -> 0.66 us
  starting transfers between devices: 10.6 us -> 0 us
  other arithmetic: 8.23 us -> 0 us
  blocking collectives: 5.92 us -> 0 us
  matrix products: 5.79 us -> 0 us
    psum x1 -> x0, waiting for transfers between devices: 112 us -> none  [per_device(): weight_grad = lax.psum(weight_term, ('blk', 'rep')) / math.sqrt(nodes)]
    pallas_call x0 -> x1, Pallas kernels: none -> 58.3 us  [per_device(): pl.pallas_call(functools.partial(kernel, dims), out_shape=(jax.ShapeDtype...]
    ppermute x6 -> x0, waiting for transfers between devices: 48.7 us -> none  [from_behind(): lax.ppermute(shard, axis, [(i, (i + by) % size) for i in range(size)])]
    reduce_scatter x2 -> x0, waiting for transfers between devices: 44.2 us -> none  [the longest x1 23.6 us: per_device(): lax.psum_scatter(partial_value, 'rep', scatter_dimension=0, tiled=True)]
    ppermute x6 -> x0, starting transfers between devices: 10.5 us -> none  [from_behind(): lax.ppermute(shard, axis, [(i, (i + by) % size) for i in range(size)])]
    unnamed x14 -> x17, local copies, waits for them, and re-layouts: 0.59 us -> 7.79 us
    reshape x2 -> x0, local copies, waits for them, and re-layouts: 7.02 us -> none  [dense_block(): placed = placed.reshape(tiles.shape[0], 128, rows_blk)]
    all_gather x1 -> x0, blocking collectives: 5.92 us -> none  [per_device(): dy_block = lax.all_gather(dy_rows, 'rep', axis=0, tiled=True)]
  transfers between devices with their start and end apart: 9 -> 0, of which waited for: 8 -> 0; matrix products, arithmetic and copies ran while one was open for 7% -> 0% of each run, Pallas kernels for 0% -> 0%
where the time goes in v1:
time: 67.1 us; the launch traced here: 66.7 us
  Pallas kernels  58.3 us (87%)
  local copies, waits for them, and re-layouts  7.79 us (12%)
    pallas_call x1, Pallas kernels, per_device(): pl.pallas_call(functools.partial(kernel, dims), out_shape=(jax.ShapeDtype...  58.3 us
    unnamed x17, local copies, waits for them, and re-layouts  7.79 us

profile of v1, /device:TPU:0, one launch (start us, length us, event | category | flops | bytes accessed | tf_op | source)
XLA Modules:
  0.0 66.7 jit_solution(13665702468350307319)
XLA Ops:
  0.6 0.0 copy-start
  0.6 1.1 %copy-done = bf16[1,2,12,128,128]{4,3,2,1,0:T(8,128)(2,1)S(1)} copy-done((bf16[1,2,12,128,128]{4,3,2,1,0:T(8,128)(2,1)S(1)}, bf16[1,2,12,128,128]{4,3,2,1,0:T(8,128)(2,1)}, u32[]{:S(2)}) %copy-start) | copy-done | bytes 786456
  1.8 0.0 copy-start.1
  1.8 0.9 %copy-done.1 = bf16[512,256]{1,0:T(8,128)(2,1)S(1)} copy-done((bf16[512,256]{1,0:T(8,128)(2,1)S(1)}, bf16[512,256]{1,0:T(8,128)(2,1)}, u32[]{:S(2)}) %copy-start.1) | copy-done | bytes 262168
  2.7 0.0 copy-start.2
  2.7 0.9 %copy-done.2 = bf16[256,256]{1,0:T(8,128)(2,1)S(1)} copy-done((bf16[256,256]{1,0:T(8,128)(2,1)S(1)}, bf16[256,256]{1,0:T(8,128)(2,1)}, u32[]{:S(2)}) %copy-start.2) | copy-done | bytes 131096
  3.6 0.0 copy-start.3
  3.6 0.8 %copy-done.3 = bf16[128,256]{1,0:T(8,128)(2,1)S(1)} copy-done((bf16[128,256]{1,0:T(8,128)(2,1)S(1)}, bf16[128,256]{1,0:T(8,128)(2,1)}, u32[]{:S(2)}) %copy-start.3) | copy-done | bytes 65560
  4.5 0.0 copy-start.4
  4.5 0.7 %copy-done.4 = s32[1,2,12]{2,1,0:T(2,128)S(1)} copy-done((s32[1,2,12]{2,1,0:T(2,128)S(1)}, s32[1,2,12]{2,1,0:T(2,128)}, u32[]{:S(2)}) %copy-start.4) | copy-done | bytes 120
  5.1 0.0 copy-start.5
  5.1 0.7 %copy-done.5 = s32[1,2,12]{2,1,0:T(2,128)S(1)} copy-done((s32[1,2,12]{2,1,0:T(2,128)S(1)}, s32[1,2,12]{2,1,0:T(2,128)}, u32[]{:S(2)}) %copy-start.5) | copy-done | bytes 120
  5.8 0.0 copy-start.6
  5.8 0.7 copy-done.6
  6.5 58.3 %graph_layer.1 = (bf16[128,256]{1,0:T(8,128)(2,1)S(1)}, f32[256,256]{1,0:T(8,128)S(1)}, bf16[128,256]{1,0:T(8,128)(2,1)S(1)}) custom-call(bf16[512,256]{1,0:T(8,128)(2,1)S(1)} %copy-done.1, bf16[256,256]{1,0:T(8,128)(2,1)S(1)} %copy-done.2, bf16[128,256]{1,0:T(8,128)(2,1)S(1)} %copy-done.3, bf16[1,2,12,128,128]{4,3,2,1,0:T(8,128)(2,1)S(1)} %copy-done, ...), custom_call_target="tpu_custom_call" | custom-call | tf_op jit(solution)/shard_map/graph_layer/pallas_call | solution.py:312
  64.7 0.6 copy.13
  65.4 0.7 %copy.14 = f32[256,256]{1,0:T(8,128)} copy(f32[256,256]{1,0:T(8,128)S(1)} %get-tuple-element.7) | data formatting | bytes 524288
  66.1 0.6 copy.15
Async XLA Ops:
  0.6 1.1 %copy-start = (bf16[1,2,12,128,128]{4,3,2,1,0:T(8,128)(2,1)S(1)}, bf16[1,2,12,128,128]{4,3,2,1,0:T(8,128)(2,1)}, u32[]{:S(2)}) copy-start(bf16[1,2,12,128,128]{4,3,2,1,0:T(8,128)(2,1)} %refs_3_.1) | copy-start | bytes 2359300
  1.8 0.9 %copy-start.1 = (bf16[512,256]{1,0:T(8,128)(2,1)S(1)}, bf16[512,256]{1,0:T(8,128)(2,1)}, u32[]{:S(2)}) copy-start(bf16[512,256]{1,0:T(8,128)(2,1)} %refs_0_.1) | copy-start | bytes 786436
  2.7 0.9 %copy-start.2 = (bf16[256,256]{1,0:T(8,128)(2,1)S(1)}, bf16[256,256]{1,0:T(8,128)(2,1)}, u32[]{:S(2)}) copy-start(bf16[256,256]{1,0:T(8,128)(2,1)} %refs_1_.1) | copy-start | bytes 393220
  3.6 0.8 %copy-start.3 = (bf16[128,256]{1,0:T(8,128)(2,1)S(1)}, bf16[128,256]{1,0:T(8,128)(2,1)}, u32[]{:S(2)}) copy-start(bf16[128,256]{1,0:T(8,128)(2,1)} %refs_2_.1) | copy-start | bytes 196612
  4.5 0.7 %copy-start.4 = (s32[1,2,12]{2,1,0:T(2,128)S(1)}, s32[1,2,12]{2,1,0:T(2,128)}, u32[]{:S(2)}) copy-start(s32[1,2,12]{2,1,0:T(2,128)} %refs_4_.1) | copy-start | bytes 292
  5.1 0.7 %copy-start.5 = (s32[1,2,12]{2,1,0:T(2,128)S(1)}, s32[1,2,12]{2,1,0:T(2,128)}, u32[]{:S(2)}) copy-start(s32[1,2,12]{2,1,0:T(2,128)} %refs_5_.1) | copy-start | bytes 292
  5.8 0.7 copy-start.6

commit v2 on v1

--- a/solution.py
+++ b/solution.py
@@ -28,14 +28,19 @@
 
 def kernel(dims, *refs):
     blocks, replicas, sections, rows_blk, width, slots, own_rows, w_rows, w_chunk, nodes = dims
-    (feat, weight, cot, tiles, trows, tcols, tcount) = refs[:7]
+    (feat, weight_hbm, cot_hbm, tiles_hbm, trows_hbm, tcols_hbm, tcount_hbm) = refs[:7]
     (act, wgrad, fgrad) = refs[7:10]
-    (fbuf, amat, amat_t, pbuf, rbuf, dzfull, agg_t, aggs, gbuf, gslots, wpart, wslots, wcol) = refs[10:23]
-    (f_send, f_recv, p_send, p_recv, z_send, z_recv, a_send, a_recv) = refs[23:31]
-    (g_send, g_recv, w_send, w_recv, c_send, c_recv, r_send, r_recv) = refs[31:]
+    (weight, cot, tiles, trows, tcols, tcount) = refs[10:16]
+    (fbuf, amat, amat_t, pbuf, rbuf, dzfull, agg_t, aggs) = refs[16:24]
+    (gsend, gpair, gbuf, gslots, wpart, wslots, wcol, l_sem) = refs[24:32]
+    (f_send, f_recv, h_send, h_recv, p_send, p_recv, z_send, z_recv, a_send, a_recv) = refs[32:42]
+    (o_send, o_recv, g_send, g_recv, w_send, w_recv, c_send, c_recv, r_send, r_recv) = refs[42:]
     b = lax.axis_index("blk")
     r = lax.axis_index("rep")
+    odd = lax.rem(b, 2)
+    pairs = sections // 2
     row_tiles = rows_blk // TILE
+    column_parts = width // TILE
     whole_weight = w_chunk > 0
 
     def blk_at(offset):
@@ -46,43 +51,87 @@
             src_ref=src, dst_ref=dst, send_sem=send, recv_sem=recv, device_id=to, device_id_type=MESH
         )
 
+    local = [
+        pltpu.make_async_copy(src, dst, l_sem.at[n])
+        for n, (src, dst) in enumerate(
+            (
+                (trows_hbm, trows),
+                (tcols_hbm, tcols),
+                (tcount_hbm, tcount),
+                (tiles_hbm, tiles),
+                (weight_hbm, weight),
+                (cot_hbm, cot),
+            )
+        )
+    ]
+    for copy in local:
+        copy.start()
+
     barrier = pltpu.get_barrier_semaphore()
 
     def greet(to):
         pl.semaphore_signal(barrier, inc=1, device_id=to, device_id_type=MESH)
 
+    neighbour = b + 1 - 2 * odd
     repeat(replicas, lambda d: greet((b, lax.rem(r + d, replicas))), 1)
     repeat(blocks, lambda d: greet((blk_at(d), r)), 1)
-
-    def greet_grad(o):
-        source = o // sections
-
-        @pl.when(jnp.logical_or(o != 0, r != 0))
+    greet((neighbour, lax.rem(r + 2 * odd - 1 + replicas, replicas)))
+
+    def greet_grad(j):
+        @pl.when(jnp.logical_or(j != 0, r != 0))
         def _():
-            greet((blk_at(-o), source))
-
-    repeat(blocks, greet_grad)
+            greet((blk_at(-2 * j), 2 * j // sections))
+
+    repeat(blocks // 2, greet_grad)
     own = jnp.where(r == 0, 1, 0)
-    pl.semaphore_wait(barrier, replicas - 1 + blocks - 1 + sections * replicas - own)
-
-    def feature_copy(s):
-        return remote(
-            feat, fbuf.at[s], f_send.at[s], f_recv.at[s], (blk_at(-(sections * r + s)), r)
-        )
-
-    for s in range(sections):
-        if s == 0:
-
-            @pl.when(r != 0)
-            def _():
-                feature_copy(0).start()
-
-            @pl.when(r == 0)
-            def _():
-                fbuf[0] = feat[...]
-        else:
-            feature_copy(s).start()
-
+    pl.semaphore_wait(barrier, replicas + blocks - 1 + pairs * replicas - own)
+
+    def columns(c):
+        return pl.ds(c * TILE, TILE)
+
+    def feature_copy(t, c):
+        return remote(
+            feat.at[:, columns(c)],
+            fbuf.at[2 * t, c],
+            f_send.at[t, c],
+            f_recv.at[t, c],
+            (blk_at(-(sections * r + 2 * t)), r),
+        )
+
+    def feature_local(c):
+        return pltpu.make_async_copy(feat.at[:, columns(c)], fbuf.at[0, c], f_recv.at[0, c])
+
+    def hand_copy(t, c):
+        section = lax.rem(2 * t + 2 * odd - 1 + sections, sections)
+        back = jnp.where(odd == 0, 1, 0) if t == 0 else 0
+        return remote(
+            fbuf.at[2 * t, c],
+            fbuf.at[section, c],
+            h_send.at[t, c],
+            h_recv.at[section // 2, c],
+            (neighbour, lax.rem(r - back + replicas, replicas)),
+        )
+
+    def hand_arrival(t, c):
+        here = fbuf.at[2 * t + 1, c]
+        return remote(here, here, h_send.at[t, c], h_recv.at[t, c], (neighbour, r))
+
+    for c in range(column_parts):
+        for t in range(pairs):
+            if t == 0:
+
+                @pl.when(r != 0)
+                def _():
+                    feature_copy(0, c).start()
+
+                @pl.when(r == 0)
+                def _():
+                    feature_local(c).start()
+            else:
+                feature_copy(t, c).start()
+
+    for copy in local[:4]:
+        copy.wait()
     for s in range(sections):
         count = tcount[0, s]
         place = [
@@ -101,45 +150,58 @@
                 amat[at_row, at_col] = tile
                 amat_t[at_col, at_row] = tile.T
 
-    for s in range(sections):
-        if s == 0:
-
-            @pl.when(r != 0)
-            def _():
-                feature_copy(0).wait()
-        else:
-            feature_copy(s).wait()
-
-    def partial_rows(k):
-        total = jnp.zeros((own_rows, width), jnp.float32)
+    for c in range(column_parts):
+        for t in range(pairs):
+            if t == 0:
+
+                @pl.when(r != 0)
+                def _():
+                    feature_copy(0, c).wait()
+
+                @pl.when(r == 0)
+                def _():
+                    feature_local(c).wait()
+            else:
+                feature_copy(t, c).wait()
+            hand_copy(t, c).start()
+
+    def partial_rows(k, c):
+        total = jnp.zeros((own_rows, TILE), jnp.float32)
         at_row = pl.ds(pl.multiple_of(k * own_rows, own_rows), own_rows)
         for s in range(sections):
             total = total + jnp.dot(
                 amat[at_row, s * rows_blk : (s + 1) * rows_blk],
-                fbuf[s],
+                fbuf[s, c],
                 preferred_element_type=jnp.float32,
             )
         return total
 
-    def partial_copy(d):
-        return remote(
-            pbuf.at[d - 1],
-            rbuf.at[d - 1],
-            p_send.at[d - 1],
-            p_recv.at[d - 1],
+    def partial_copy(d, c):
+        return remote(
+            pbuf.at[d - 1, c],
+            rbuf.at[d - 1, c],
+            p_send.at[d - 1, c],
+            p_recv.at[d - 1, c],
             (b, lax.rem(r + d, replicas)),
         )
 
-    def send_partial(d):
-        pbuf[d - 1] = partial_rows(lax.rem(r + d, replicas)).astype(pbuf.dtype)
-        partial_copy(d).start()
-
-    repeat(replicas, send_partial, 1)
-    total = partial_rows(r)
-    repeat(replicas, lambda d: partial_copy(d).wait(), 1)
-    for d in range(1, replicas):
-        total = total + rbuf[d - 1].astype(jnp.float32)
-    agg = total.astype(jnp.bfloat16)
+    def send_partial(d, c):
+        pbuf[d - 1, c] = partial_rows(lax.rem(r + d, replicas), c).astype(pbuf.dtype)
+        partial_copy(d, c).start()
+
+    totals = []
+    for c in range(column_parts):
+        for t in range(pairs):
+            hand_arrival(t, c).wait_recv()
+        repeat(replicas, lambda d: send_partial(d, c), 1)
+        totals.append(partial_rows(r, c))
+    for copy in local[4:]:
+        copy.wait()
+    for c in range(column_parts):
+        repeat(replicas, lambda d: partial_copy(d, c).wait(), 1)
+        for d in range(1, replicas):
+            totals[c] = totals[c] + rbuf[d - 1, c].astype(jnp.float32)
+    agg = jnp.concatenate(totals, axis=1).astype(jnp.bfloat16)
 
     z_value = jnp.dot(agg, weight[...], preferred_element_type=jnp.float32)
     sigma = jax.nn.sigmoid(z_value)
@@ -180,28 +242,46 @@
         dzfull[...], weight[...], (((1,), (1,)), ((), ())), preferred_element_type=jnp.float32
     ).astype(jnp.bfloat16)
 
-    def grad_copy(s, k):
-        o = sections * r + s
-        return remote(
-            gbuf.at[s, k], gslots.at[o], g_send.at[s, k], g_recv.at[o], (blk_at(o), k)
-        )
-
-    def send_grad(s, k):
+    def grad_rows(s, k):
         at_row = pl.ds(s * rows_blk + k * own_rows, own_rows)
-        gbuf[s, k] = jnp.dot(amat_t[at_row, :], dy, preferred_element_type=jnp.float32).astype(
-            gbuf.dtype
-        )
-        if s == 0 and k == 0:
+        return jnp.dot(amat_t[at_row, :], dy, preferred_element_type=jnp.float32)
+
+    def odd_copy(t, k):
+        slot = lax.rem(t + odd, pairs)
+        ahead = odd if t == pairs - 1 else 0
+        return remote(
+            gsend.at[t, k],
+            gpair.at[slot, k],
+            o_send.at[t, k],
+            o_recv.at[slot, k],
+            (neighbour, lax.rem(r + ahead, replicas)),
+        )
+
+    def odd_arrival(t, k):
+        here = gpair.at[t, k]
+        return remote(here, here, o_send.at[t, k], o_recv.at[t, k], (neighbour, r))
+
+    def grad_copy(t, k):
+        j = pairs * r + t
+        return remote(
+            gbuf.at[t, k], gslots.at[j], g_send.at[t, k], g_recv.at[j], (blk_at(2 * j), k)
+        )
+
+    def send_grad(t, k):
+        term = grad_rows(2 * t, k)
+        odd_arrival(t, k).wait_recv()
+        gbuf[t, k] = (term + gpair[t, k].astype(jnp.float32)).astype(gbuf.dtype)
+        if t == 0 and k == 0:
 
             @pl.when(r != 0)
             def _():
-                grad_copy(s, k).start()
+                grad_copy(t, k).start()
 
             @pl.when(r == 0)
             def _():
                 gslots[0] = gbuf[0, 0]
         else:
-            grad_copy(s, k).start()
+            grad_copy(t, k).start()
 
     def weight_rows():
         repeat(replicas, lambda d: agg_copy(d).wait_recv(), 1)
@@ -240,15 +320,20 @@
         at_row = pl.ds(pl.multiple_of(source * w_rows, w_rows), w_rows)
         return remote(wcol, wgrad.at[at_row], r_send.at[d - 1], r_recv.at[d - 1], (b, source))
 
+    for t in range(pairs):
+        for k in range(replicas):
+            gsend[t, k] = grad_rows(2 * t + 1, k).astype(gsend.dtype)
+            odd_copy(t, k).start()
+
     if whole_weight:
         wpart[...] = weight_rows()
         repeat(blocks, lambda d: w_copy(d).start(), 1)
     else:
         wgrad[...] = weight_rows()
 
-    for s in reversed(range(sections)):
+    for t in range(pairs):
         for k in range(replicas):
-            send_grad(s, k)
+            send_grad(t, k)
 
     if whole_weight:
         repeat(blocks, lambda d: w_copy(d).wait_recv(), 1)
@@ -261,32 +346,36 @@
         repeat(replicas, lambda d: r_copy(d).start(), 1)
         wgrad[pl.ds(pl.multiple_of(r * w_rows, w_rows), w_rows), :] = wcol[...]
 
-    def grad_arrival(o):
+    def grad_arrival(j):
         copy = remote(
-            gslots.at[o], gslots.at[o], g_send.at[0, 0], g_recv.at[o], (blk_at(-o), o // sections)
-        )
-
-        @pl.when(jnp.logical_or(o != 0, r != 0))
+            gslots.at[j], gslots.at[j], g_send.at[0, 0], g_recv.at[j], (blk_at(-2 * j), j // pairs)
+        )
+
+        @pl.when(jnp.logical_or(j != 0, r != 0))
         def _():
             copy.wait_recv()
 
-    repeat(blocks, grad_arrival)
+    repeat(blocks // 2, grad_arrival)
     summed = gslots[0].astype(jnp.float32)
-    for o in range(1, blocks):
-        summed = summed + gslots[o].astype(jnp.float32)
+    for j in range(1, blocks // 2):
+        summed = summed + gslots[j].astype(jnp.float32)
     fgrad[...] = summed.astype(jnp.bfloat16)
 
+    for t in range(pairs):
+        for c in range(column_parts):
+            hand_copy(t, c).wait_send()
     repeat(replicas, lambda d: dz_copy(d).wait_send(), 1)
     repeat(replicas, lambda d: agg_copy(d).wait_send(), 1)
-    for s in range(sections):
+    for t in range(pairs):
         for k in range(replicas):
-            if s == 0 and k == 0:
+            odd_copy(t, k).wait_send()
+            if t == 0 and k == 0:
 
                 @pl.when(r != 0)
                 def _():
-                    grad_copy(s, k).wait_send()
+                    grad_copy(t, k).wait_send()
             else:
-                grad_copy(s, k).wait_send()
+                grad_copy(t, k).wait_send()
     if whole_weight:
         repeat(blocks, lambda d: w_copy(d).wait_send(), 1)
         repeat(blocks, lambda d: c_copy(d).wait_send(), 1)
@@ -306,9 +395,9 @@
     dims = (blocks, replicas, sections, rows_blk, width, slots, own_rows, w_rows, w_chunk, nodes)
     bf16, f32 = jnp.bfloat16, jnp.float32
     vmem = pl.BlockSpec(memory_space=pltpu.VMEM)
-    smem = pl.BlockSpec(memory_space=pltpu.SMEM)
     dma = pltpu.SemaphoreType.DMA
     others = max(replicas - 1, 1)
+    pairs, parts = sections // 2, width // TILE
     act, wgrad, fgrad = pl.pallas_call(
         functools.partial(kernel, dims),
         out_shape=(
@@ -316,41 +405,54 @@
             jax.ShapeDtypeStruct((width if w_chunk else w_rows, width), f32),
             jax.ShapeDtypeStruct((own_rows, width), bf16),
         ),
-        in_specs=[vmem] * 4 + [smem] * 3,
+        in_specs=[pl.BlockSpec(memory_space=pl.ANY)] * 7,
         out_specs=(vmem, vmem, vmem),
         scratch_shapes=[
-            pltpu.VMEM((sections, rows_blk, width), bf16),
+            pltpu.VMEM(weight.shape, bf16),
+            pltpu.VMEM(cotangent.shape, bf16),
+            pltpu.VMEM(tile_values.shape, bf16),
+            pltpu.SMEM(tile_rows.shape, jnp.int32),
+            pltpu.SMEM(tile_cols.shape, jnp.int32),
+            pltpu.SMEM(tile_count.shape, jnp.int32),
+            pltpu.VMEM((sections, parts, rows_blk, TILE), bf16),
             pltpu.VMEM((rows_blk, sections * rows_blk), bf16),
             pltpu.VMEM((sections * rows_blk, rows_blk), bf16),
-            pltpu.VMEM((others, own_rows, width), bf16),
-            pltpu.VMEM((others, own_rows, width), bf16),
+            pltpu.VMEM((others, parts, own_rows, TILE), bf16),
+            pltpu.VMEM((others, parts, own_rows, TILE), bf16),
             pltpu.VMEM((rows_blk, width), bf16),
             pltpu.VMEM((width, own_rows), bf16),
             pltpu.VMEM((replicas, w_rows, own_rows), bf16),
-            pltpu.VMEM((sections, replicas, own_rows, width), bf16),
-            pltpu.VMEM((blocks, own_rows, width), bf16),
+            pltpu.VMEM((pairs, replicas, own_rows, width), bf16),
+            pltpu.VMEM((pairs, replicas, own_rows, width), bf16),
+            pltpu.VMEM((pairs, replicas, own_rows, width), bf16),
+            pltpu.VMEM((blocks // 2, own_rows, width), bf16),
             pltpu.VMEM((w_rows, width), f32),
             pltpu.VMEM((blocks, max(w_chunk, 8), width), f32),
             pltpu.VMEM((w_rows, width), f32),
-            dma((sections,)),
-            dma((sections,)),
-            dma((others,)),
-            dma((others,)),
-            dma((others,)),
-            dma((others,)),
-            dma((others,)),
-            dma((others,)),
-            dma((sections, replicas)),
+            dma((6,)),
+            dma((pairs, parts)),
+            dma((pairs, parts)),
+            dma((pairs, parts)),
+            dma((pairs, parts)),
+            dma((others, parts)),
+            dma((others, parts)),
+            dma((others,)),
+            dma((others,)),
+            dma((others,)),
+            dma((others,)),
+            dma((pairs, replicas)),
+            dma((pairs, replicas)),
+            dma((pairs, replicas)),
+            dma((blocks // 2,)),
             dma((blocks,)),
             dma((blocks,)),
             dma((blocks,)),
             dma((blocks,)),
-            dma((blocks,)),
             dma((others,)),
             dma((others,)),
         ],
         compiler_params=pltpu.CompilerParams(
-            collective_id=0, has_side_effects=True, vmem_limit_bytes=24 * 1024 * 1024
+            collective_id=0, has_side_effects=True, vmem_limit_bytes=48 * 1024 * 1024
         ),
         name="graph_layer",
     )(features, weight, cotangent, tile_values, tile_rows, tile_cols, tile_count)

time: 67.1 us -> 57.8 us (0.86)
  Pallas kernels: 58.3 us -> 48.3 us
    pallas_call x1, Pallas kernels: 58.3 us -> 48.3 us  [per_device(): pl.pallas_call(functools.partial(kernel, dims), out_shape=(jax.ShapeDtype...]
where the time goes in v2:
time: 57.8 us; the launch traced here: 56.8 us
  Pallas kernels  48.3 us (84%)
  local copies, waits for them, and re-layouts  7.79 us (13%)
  between operations  0.66 us (1%)
    pallas_call x1, Pallas kernels, per_device(): pl.pallas_call(functools.partial(kernel, dims), out_shape=(jax.ShapeDtype...  48.3 us
    unnamed x17, local copies, waits for them, and re-layouts  7.79 us

profile of v2, /device:TPU:0, one launch (start us, length us, event | category | flops | bytes accessed | tf_op | source)
XLA Modules:
  0.0 56.8 jit_solution(17125505424622086385)
XLA Ops:
  0.6 0.0 copy-start
  0.6 1.1 %copy-done = bf16[1,2,12,128,128]{4,3,2,1,0:T(8,128)(2,1)S(1)} copy-done((bf16[1,2,12,128,128]{4,3,2,1,0:T(8,128)(2,1)S(1)}, bf16[1,2,12,128,128]{4,3,2,1,0:T(8,128)(2,1)}, u32[]{:S(2)}) %copy-start) | copy-done | bytes 786456
  1.8 0.0 copy-start.1
  1.8 0.9 %copy-done.1 = bf16[512,256]{1,0:T(8,128)(2,1)S(1)} copy-done((bf16[512,256]{1,0:T(8,128)(2,1)S(1)}, bf16[512,256]{1,0:T(8,128)(2,1)}, u32[]{:S(2)}) %copy-start.1) | copy-done | bytes 262168
  2.7 0.0 copy-start.2
  2.7 0.9 %copy-done.2 = bf16[256,256]{1,0:T(8,128)(2,1)S(1)} copy-done((bf16[256,256]{1,0:T(8,128)(2,1)S(1)}, bf16[256,256]{1,0:T(8,128)(2,1)}, u32[]{:S(2)}) %copy-start.2) | copy-done | bytes 131096
  3.6 0.0 copy-start.3
  3.6 0.8 %copy-done.3 = bf16[128,256]{1,0:T(8,128)(2,1)S(1)} copy-done((bf16[128,256]{1,0:T(8,128)(2,1)S(1)}, bf16[128,256]{1,0:T(8,128)(2,1)}, u32[]{:S(2)}) %copy-start.3) | copy-done | bytes 65560
  4.5 0.0 copy-start.4
  4.5 0.7 %copy-done.4 = s32[1,2,12]{2,1,0:T(2,128)S(1)} copy-done((s32[1,2,12]{2,1,0:T(2,128)S(1)}, s32[1,2,12]{2,1,0:T(2,128)}, u32[]{:S(2)}) %copy-start.4) | copy-done | bytes 120
  5.1 0.0 copy-start.5
  5.1 0.7 %copy-done.5 = s32[1,2,12]{2,1,0:T(2,128)S(1)} copy-done((s32[1,2,12]{2,1,0:T(2,128)S(1)}, s32[1,2,12]{2,1,0:T(2,128)}, u32[]{:S(2)}) %copy-start.5) | copy-done | bytes 120
  5.8 0.0 copy-start.6
  5.8 0.7 %copy-done.6 = s32[1,2]{1,0:T(1,128)S(1)} copy-done((s32[1,2]{1,0:T(1,128)S(1)}, s32[1,2]{1,0:T(1,128)}, u32[]{:S(2)}) %copy-start.6) | copy-done | bytes 32
  6.5 48.3 %graph_layer.1 = (bf16[128,256]{1,0:T(8,128)(2,1)S(1)}, f32[256,256]{1,0:T(8,128)S(1)}, bf16[128,256]{1,0:T(8,128)(2,1)S(1)}) custom-call(bf16[512,256]{1,0:T(8,128)(2,1)S(1)} %copy-done.1, bf16[256,256]{1,0:T(8,128)(2,1)S(1)} %copy-done.2, bf16[128,256]{1,0:T(8,128)(2,1)S(1)} %copy-done.3, bf16[1,2,12,128,128]{4,3,2,1,0:T(8,128)(2,1)S(1)} %copy-done, ...), custom_call_target="tpu_custom_call" | custom-call | tf_op jit(solution)/shard_map/graph_layer/pallas_call | solution.py:401
  54.8 0.6 %copy.13 = bf16[128,256]{1,0:T(8,128)(2,1)} copy(bf16[128,256]{1,0:T(8,128)(2,1)S(1)} %get-tuple-element.6) | data formatting | bytes 131072
  55.5 0.7 %copy.14 = f32[256,256]{1,0:T(8,128)} copy(f32[256,256]{1,0:T(8,128)S(1)} %get-tuple-element.7) | data formatting | bytes 524288
  56.2 0.6 %copy.15 = bf16[128,256]{1,0:T(8,128)(2,1)} copy(bf16[128,256]{1,0:T(8,128)(2,1)S(1)} %get-tuple-element.8) | data formatting | bytes 131072
Async XLA Ops:
  0.6 1.1 %copy-start = (bf16[1,2,12,128,128]{4,3,2,1,0:T(8,128)(2,1)S(1)}, bf16[1,2,12,128,128]{4,3,2,1,0:T(8,128)(2,1)}, u32[]{:S(2)}) copy-start(bf16[1,2,12,128,128]{4,3,2,1,0:T(8,128)(2,1)} %refs_3_.1) | copy-start | bytes 2359300
  1.8 0.9 %copy-start.1 = (bf16[512,256]{1,0:T(8,128)(2,1)S(1)}, bf16[512,256]{1,0:T(8,128)(2,1)}, u32[]{:S(2)}) copy-start(bf16[512,256]{1,0:T(8,128)(2,1)} %refs_0_.1) | copy-start | bytes 786436
  2.7 0.9 %copy-start.2 = (bf16[256,256]{1,0:T(8,128)(2,1)S(1)}, bf16[256,256]{1,0:T(8,128)(2,1)}, u32[]{:S(2)}) copy-start(bf16[256,256]{1,0:T(8,128)(2,1)} %refs_1_.1) | copy-start | bytes 393220
  3.6 0.8 %copy-start.3 = (bf16[128,256]{1,0:T(8,128)(2,1)S(1)}, bf16[128,256]{1,0:T(8,128)(2,1)}, u32[]{:S(2)}) copy-start(bf16[128,256]{1,0:T(8,128)(2,1)} %refs_2_.1) | copy-start | bytes 196612
  4.5 0.7 %copy-start.4 = (s32[1,2,12]{2,1,0:T(2,128)S(1)}, s32[1,2,12]{2,1,0:T(2,128)}, u32[]{:S(2)}) copy-start(s32[1,2,12]{2,1,0:T(2,128)} %refs_4_.1) | copy-start | bytes 292
  5.1 0.7 %copy-start.5 = (s32[1,2,12]{2,1,0:T(2,128)S(1)}, s32[1,2,12]{2,1,0:T(2,128)}, u32[]{:S(2)}) copy-start(s32[1,2,12]{2,1,0:T(2,128)} %refs_5_.1) | copy-start | bytes 292
  5.8 0.7 %copy-start.6 = (s32[1,2]{1,0:T(1,128)S(1)}, s32[1,2]{1,0:T(1,128)}, u32[]{:S(2)}) copy-start(s32[1,2]{1,0:T(1,128)} %refs_6_.1) | copy-start | bytes 28

commit v3 on v2

--- a/solution.py
+++ b/solution.py
@@ -11,6 +11,7 @@
 MESH = pl.DeviceIdType.MESH
 TILE = 128
 UNROLL = 8
+HALVES = 2
 
 
 def repeat(count, body, first=0):
@@ -32,9 +33,10 @@
     (act, wgrad, fgrad) = refs[7:10]
     (weight, cot, tiles, trows, tcols, tcount) = refs[10:16]
     (fbuf, amat, amat_t, pbuf, rbuf, dzfull, agg_t, aggs) = refs[16:24]
-    (gsend, gpair, gbuf, gslots, wpart, wslots, wcol, l_sem) = refs[24:32]
-    (f_send, f_recv, h_send, h_recv, p_send, p_recv, z_send, z_recv, a_send, a_recv) = refs[32:42]
-    (o_send, o_recv, g_send, g_recv, w_send, w_recv, c_send, c_recv, r_send, r_recv) = refs[42:]
+    (gsend, gpair, gbuf, gslots, wpart, wslots, wcol) = refs[24:31]
+    (pfull, weight_t, gterm, l_sem) = refs[31:35]
+    (f_send, f_recv, h_send, h_recv, p_send, p_recv, z_send, z_recv, a_send, a_recv) = refs[35:45]
+    (o_send, o_recv, g_send, g_recv, w_send, w_recv, c_send, c_recv, r_send, r_recv) = refs[45:]
     b = lax.axis_index("blk")
     r = lax.axis_index("rep")
     odd = lax.rem(b, 2)
@@ -42,6 +44,7 @@
     row_tiles = rows_blk // TILE
     column_parts = width // TILE
     whole_weight = w_chunk > 0
+    pieces = [(c, h) for c in range(column_parts) for h in range(HALVES)]
 
     def blk_at(offset):
         return lax.rem(b + offset + 2 * blocks, blocks)
@@ -86,53 +89,59 @@
     own = jnp.where(r == 0, 1, 0)
     pl.semaphore_wait(barrier, replicas + blocks - 1 + pairs * replicas - own)
 
-    def columns(c):
-        return pl.ds(c * TILE, TILE)
-
-    def feature_copy(t, c):
-        return remote(
-            feat.at[:, columns(c)],
-            fbuf.at[2 * t, c],
-            f_send.at[t, c],
-            f_recv.at[t, c],
+    half_rows = rows_blk // HALVES
+
+    def piece(section, c, h):
+        return fbuf.at[section, c, pl.ds(h * half_rows, half_rows)]
+
+    def feature_piece(c, h):
+        return feat.at[pl.ds(h * half_rows, half_rows), pl.ds(c * TILE, TILE)]
+
+    def feature_copy(t, c, h):
+        return remote(
+            feature_piece(c, h),
+            piece(2 * t, c, h),
+            f_send.at[t, c, h],
+            f_recv.at[t, c, h],
             (blk_at(-(sections * r + 2 * t)), r),
         )
 
-    def feature_local(c):
-        return pltpu.make_async_copy(feat.at[:, columns(c)], fbuf.at[0, c], f_recv.at[0, c])
-
-    def hand_copy(t, c):
+    def feature_local(c, h):
+        return pltpu.make_async_copy(feature_piece(c, h), piece(0, c, h), f_recv.at[0, c, h])
+
+    def hand_copy(t, c, h):
         section = lax.rem(2 * t + 2 * odd - 1 + sections, sections)
         back = jnp.where(odd == 0, 1, 0) if t == 0 else 0
         return remote(
-            fbuf.at[2 * t, c],
-            fbuf.at[section, c],
-            h_send.at[t, c],
-            h_recv.at[section // 2, c],
+            piece(2 * t, c, h),
+            piece(section, c, h),
+            h_send.at[t, c, h],
+            h_recv.at[section // 2, c, h],
             (neighbour, lax.rem(r - back + replicas, replicas)),
         )
 
-    def hand_arrival(t, c):
-        here = fbuf.at[2 * t + 1, c]
-        return remote(here, here, h_send.at[t, c], h_recv.at[t, c], (neighbour, r))
-
-    for c in range(column_parts):
+    def hand_arrival(t, c, h):
+        here = piece(2 * t + 1, c, h)
+        return remote(here, here, h_send.at[t, c, h], h_recv.at[t, c, h], (neighbour, r))
+
+    for c, h in pieces:
         for t in range(pairs):
             if t == 0:
 
                 @pl.when(r != 0)
                 def _():
-                    feature_copy(0, c).start()
+                    feature_copy(0, c, h).start()
 
                 @pl.when(r == 0)
                 def _():
-                    feature_local(c).start()
+                    feature_local(c, h).start()
             else:
-                feature_copy(t, c).start()
+                feature_copy(t, c, h).start()
 
     for copy in local[:4]:
         copy.wait()
-    for s in range(sections):
+
+    def place_tiles(s):
         count = tcount[0, s]
         place = [
             jnp.where(t < count, trows[0, s, t] * row_tiles + tcols[0, s, t], -1)
@@ -145,58 +154,70 @@
                     slot = jnp.where(place[t] == i * row_tiles + j, t + 1, slot)
                 tile = tiles[0, s, jnp.maximum(slot - 1, 0)]
                 tile = jnp.where(slot > 0, tile, jnp.zeros_like(tile))
+                at_col = pl.ds(s * rows_blk + j * TILE, TILE)
+                amat[pl.ds(i * TILE, TILE), at_col] = tile
+
+    def turn_tiles(s):
+        for i in range(row_tiles):
+            for j in range(row_tiles):
                 at_row = pl.ds(i * TILE, TILE)
                 at_col = pl.ds(s * rows_blk + j * TILE, TILE)
-                amat[at_row, at_col] = tile
-                amat_t[at_col, at_row] = tile.T
-
-    for c in range(column_parts):
+                amat_t[at_col, at_row] = amat[at_row, at_col].T
+
+    for s in range(pairs):
+        place_tiles(s)
+    for n, (c, h) in enumerate(pieces):
         for t in range(pairs):
             if t == 0:
 
                 @pl.when(r != 0)
                 def _():
-                    feature_copy(0, c).wait()
+                    feature_copy(0, c, h).wait()
 
                 @pl.when(r == 0)
                 def _():
-                    feature_local(c).wait()
+                    feature_local(c, h).wait()
             else:
-                feature_copy(t, c).wait()
-            hand_copy(t, c).start()
-
-    def partial_rows(k, c):
-        total = jnp.zeros((own_rows, TILE), jnp.float32)
-        at_row = pl.ds(pl.multiple_of(k * own_rows, own_rows), own_rows)
+                feature_copy(t, c, h).wait()
+            hand_copy(t, c, h).start()
+        if n == 0:
+            for s in range(pairs, sections):
+                place_tiles(s)
+
+    def rows_of(k):
+        return pl.ds(pl.multiple_of(k * own_rows, own_rows), own_rows)
+
+    def partial_copy(d, c):
+        peer = lax.rem(r + d, replicas)
+        return remote(
+            pbuf.at[c, rows_of(peer)],
+            rbuf.at[d - 1, c],
+            p_send.at[d - 1, c],
+            p_recv.at[d - 1, c],
+            (b, peer),
+        )
+
+    totals = []
+    for c in range(column_parts):
+        for h in range(HALVES):
+            for t in range(pairs):
+                hand_arrival(t, c, h).wait_recv()
+        product = jnp.zeros((rows_blk, TILE), jnp.float32)
         for s in range(sections):
-            total = total + jnp.dot(
-                amat[at_row, s * rows_blk : (s + 1) * rows_blk],
+            product = product + jnp.dot(
+                amat[:, s * rows_blk : (s + 1) * rows_blk],
                 fbuf[s, c],
                 preferred_element_type=jnp.float32,
             )
-        return total
-
-    def partial_copy(d, c):
-        return remote(
-            pbuf.at[d - 1, c],
-            rbuf.at[d - 1, c],
-            p_send.at[d - 1, c],
-            p_recv.at[d - 1, c],
-            (b, lax.rem(r + d, replicas)),
-        )
-
-    def send_partial(d, c):
-        pbuf[d - 1, c] = partial_rows(lax.rem(r + d, replicas), c).astype(pbuf.dtype)
-        partial_copy(d, c).start()
-
-    totals = []
-    for c in range(column_parts):
-        for t in range(pairs):
-            hand_arrival(t, c).wait_recv()
-        repeat(replicas, lambda d: send_partial(d, c), 1)
-        totals.append(partial_rows(r, c))
+        pbuf[c] = product.astype(pbuf.dtype)
+        repeat(replicas, lambda d: partial_copy(d, c).start(), 1)
+        pfull[...] = product
+        totals.append(pfull[rows_of(r), :])
+    for s in range(1, sections, 2):
+        turn_tiles(s)
     for copy in local[4:]:
         copy.wait()
+    weight_t[...] = weight[...].T
     for c in range(column_parts):
         repeat(replicas, lambda d: partial_copy(d, c).wait(), 1)
         for d in range(1, replicas):
@@ -236,14 +257,14 @@
     repeat(replicas, lambda d: agg_copy(d).start(), 1)
     aggs[0] = agg_t[pl.ds(pl.multiple_of(r * w_rows, w_rows), w_rows), :]
     act[...] = (z_value * sigma).astype(jnp.bfloat16)
+    for s in range(0, sections, 2):
+        turn_tiles(s)
 
     repeat(replicas, lambda d: dz_arrival(d).wait_recv(), 1)
-    dy = lax.dot_general(
-        dzfull[...], weight[...], (((1,), (1,)), ((), ())), preferred_element_type=jnp.float32
-    ).astype(jnp.bfloat16)
-
-    def grad_rows(s, k):
-        at_row = pl.ds(s * rows_blk + k * own_rows, own_rows)
+    dy = jnp.dot(dzfull[...], weight_t[...], preferred_element_type=jnp.float32).astype(jnp.bfloat16)
+
+    def grad_terms(s):
+        at_row = pl.ds(s * rows_blk, rows_blk)
         return jnp.dot(amat_t[at_row, :], dy, preferred_element_type=jnp.float32)
 
     def odd_copy(t, k):
@@ -268,7 +289,7 @@
         )
 
     def send_grad(t, k):
-        term = grad_rows(2 * t, k)
+        term = gterm[t, k]
         odd_arrival(t, k).wait_recv()
         gbuf[t, k] = (term + gpair[t, k].astype(jnp.float32)).astype(gbuf.dtype)
         if t == 0 and k == 0:
@@ -321,9 +342,11 @@
         return remote(wcol, wgrad.at[at_row], r_send.at[d - 1], r_recv.at[d - 1], (b, source))
 
     for t in range(pairs):
+        gsend[t] = grad_terms(2 * t + 1).astype(gsend.dtype).reshape(gsend.shape[1:])
         for k in range(replicas):
-            gsend[t, k] = grad_rows(2 * t + 1, k).astype(gsend.dtype)
             odd_copy(t, k).start()
+    for t in range(pairs):
+        gterm[t] = grad_terms(2 * t).reshape(gterm.shape[1:])
 
     if whole_weight:
         wpart[...] = weight_rows()
@@ -362,8 +385,8 @@
     fgrad[...] = summed.astype(jnp.bfloat16)
 
     for t in range(pairs):
-        for c in range(column_parts):
-            hand_copy(t, c).wait_send()
+        for c, h in pieces:
+            hand_copy(t, c, h).wait_send()
     repeat(replicas, lambda d: dz_copy(d).wait_send(), 1)
     repeat(replicas, lambda d: agg_copy(d).wait_send(), 1)
     for t in range(pairs):
@@ -405,7 +428,7 @@
             jax.ShapeDtypeStruct((width if w_chunk else w_rows, width), f32),
             jax.ShapeDtypeStruct((own_rows, width), bf16),
         ),
-        in_specs=[pl.BlockSpec(memory_space=pl.ANY)] * 7,
+        in_specs=[pl.BlockSpec(memory_space=pltpu.HBM)] * 7,
         out_specs=(vmem, vmem, vmem),
         scratch_shapes=[
             pltpu.VMEM(weight.shape, bf16),
@@ -417,7 +440,7 @@
             pltpu.VMEM((sections, parts, rows_blk, TILE), bf16),
             pltpu.VMEM((rows_blk, sections * rows_blk), bf16),
             pltpu.VMEM((sections * rows_blk, rows_blk), bf16),
-            pltpu.VMEM((others, parts, own_rows, TILE), bf16),
+            pltpu.VMEM((parts, rows_blk, TILE), bf16),
             pltpu.VMEM((others, parts, own_rows, TILE), bf16),
             pltpu.VMEM((rows_blk, width), bf16),
             pltpu.VMEM((width, own_rows), bf16),
@@ -429,11 +452,14 @@
             pltpu.VMEM((w_rows, width), f32),
             pltpu.VMEM((blocks, max(w_chunk, 8), width), f32),
             pltpu.VMEM((w_rows, width), f32),
+            pltpu.VMEM((rows_blk, TILE), f32),
+            pltpu.VMEM(weight.shape, bf16),
+            pltpu.VMEM((pairs, replicas, own_rows, width), f32),
             dma((6,)),
-            dma((pairs, parts)),
-            dma((pairs, parts)),
-            dma((pairs, parts)),
-            dma((pairs, parts)),
+            dma((pairs, parts, HALVES)),
+            dma((pairs, parts, HALVES)),
+            dma((pairs, parts, HALVES)),
+            dma((pairs, parts, HALVES)),
             dma((others, parts)),
             dma((others, parts)),
             dma((others,)),

time: 57.8 us -> 56.9 us (0.984)
  no operation moved by 1% of the time
where the time goes in v3:
time: 56.9 us; the launch traced here: 56.3 us
  Pallas kernels  47.9 us (84%)
  local copies, waits for them, and re-layouts  7.79 us (14%)
  between operations  0.66 us (1%)
    pallas_call x1, Pallas kernels, per_device(): pl.pallas_call(functools.partial(kernel, dims), out_shape=(jax.ShapeDtype...  47.9 us
    unnamed x17, local copies, waits for them, and re-layouts  7.79 us

profile of v3, /device:TPU:0, one launch (start us, length us, event | category | flops | bytes accessed | tf_op | source)
XLA Modules:
  0.0 56.3 jit_solution(17097260002403754538)
XLA Ops:
  0.6 0.0 copy-start
  0.6 1.1 %copy-done = bf16[1,2,12,128,128]{4,3,2,1,0:T(8,128)(2,1)S(1)} copy-done((bf16[1,2,12,128,128]{4,3,2,1,0:T(8,128)(2,1)S(1)}, bf16[1,2,12,128,128]{4,3,2,1,0:T(8,128)(2,1)}, u32[]{:S(2)}) %copy-start) | copy-done | bytes 786456
  1.8 0.0 copy-start.1
  1.8 0.9 %copy-done.1 = bf16[512,256]{1,0:T(8,128)(2,1)S(1)} copy-done((bf16[512,256]{1,0:T(8,128)(2,1)S(1)}, bf16[512,256]{1,0:T(8,128)(2,1)}, u32[]{:S(2)}) %copy-start.1) | copy-done | bytes 262168
  2.7 0.0 copy-start.2
  2.7 0.9 %copy-done.2 = bf16[256,256]{1,0:T(8,128)(2,1)S(1)} copy-done((bf16[256,256]{1,0:T(8,128)(2,1)S(1)}, bf16[256,256]{1,0:T(8,128)(2,1)}, u32[]{:S(2)}) %copy-start.2) | copy-done | bytes 131096
  3.6 0.0 copy-start.3
  3.6 0.8 %copy-done.3 = bf16[128,256]{1,0:T(8,128)(2,1)S(1)} copy-done((bf16[128,256]{1,0:T(8,128)(2,1)S(1)}, bf16[128,256]{1,0:T(8,128)(2,1)}, u32[]{:S(2)}) %copy-start.3) | copy-done | bytes 65560
  4.5 0.0 copy-start.4
  4.5 0.7 %copy-done.4 = s32[1,2,12]{2,1,0:T(2,128)S(1)} copy-done((s32[1,2,12]{2,1,0:T(2,128)S(1)}, s32[1,2,12]{2,1,0:T(2,128)}, u32[]{:S(2)}) %copy-start.4) | copy-done | bytes 120
  5.1 0.0 copy-start.5
  5.1 0.7 %copy-done.5 = s32[1,2,12]{2,1,0:T(2,128)S(1)} copy-done((s32[1,2,12]{2,1,0:T(2,128)S(1)}, s32[1,2,12]{2,1,0:T(2,128)}, u32[]{:S(2)}) %copy-start.5) | copy-done | bytes 120
  5.8 0.0 copy-start.6
  5.8 0.7 %copy-done.6 = s32[1,2]{1,0:T(1,128)S(1)} copy-done((s32[1,2]{1,0:T(1,128)S(1)}, s32[1,2]{1,0:T(1,128)}, u32[]{:S(2)}) %copy-start.6) | copy-done | bytes 32
  6.5 47.9 %graph_layer.1 = (bf16[128,256]{1,0:T(8,128)(2,1)S(1)}, f32[256,256]{1,0:T(8,128)S(1)}, bf16[128,256]{1,0:T(8,128)(2,1)S(1)}) custom-call(bf16[512,256]{1,0:T(8,128)(2,1)S(1)} %copy-done.1, bf16[256,256]{1,0:T(8,128)(2,1)S(1)} %copy-done.2, bf16[128,256]{1,0:T(8,128)(2,1)S(1)} %copy-done.3, bf16[1,2,12,128,128]{4,3,2,1,0:T(8,128)(2,1)S(1)} %copy-done, ...), custom_call_target="tpu_custom_call" | custom-call | tf_op jit(solution)/shard_map/graph_layer/pallas_call | solution.py:424
  54.4 0.6 %copy.13 = bf16[128,256]{1,0:T(8,128)(2,1)} copy(bf16[128,256]{1,0:T(8,128)(2,1)S(1)} %get-tuple-element.6) | data formatting | bytes 131072
  55.0 0.7 %copy.14 = f32[256,256]{1,0:T(8,128)} copy(f32[256,256]{1,0:T(8,128)S(1)} %get-tuple-element.7) | data formatting | bytes 524288
  55.7 0.6 %copy.15 = bf16[128,256]{1,0:T(8,128)(2,1)} copy(bf16[128,256]{1,0:T(8,128)(2,1)S(1)} %get-tuple-element.8) | data formatting | bytes 131072
Async XLA Ops:
  0.6 1.1 %copy-start = (bf16[1,2,12,128,128]{4,3,2,1,0:T(8,128)(2,1)S(1)}, bf16[1,2,12,128,128]{4,3,2,1,0:T(8,128)(2,1)}, u32[]{:S(2)}) copy-start(bf16[1,2,12,128,128]{4,3,2,1,0:T(8,128)(2,1)} %refs_3_.1) | copy-start | bytes 2359300
  1.8 0.9 %copy-start.1 = (bf16[512,256]{1,0:T(8,128)(2,1)S(1)}, bf16[512,256]{1,0:T(8,128)(2,1)}, u32[]{:S(2)}) copy-start(bf16[512,256]{1,0:T(8,128)(2,1)} %refs_0_.1) | copy-start | bytes 786436
  2.7 0.9 %copy-start.2 = (bf16[256,256]{1,0:T(8,128)(2,1)S(1)}, bf16[256,256]{1,0:T(8,128)(2,1)}, u32[]{:S(2)}) copy-start(bf16[256,256]{1,0:T(8,128)(2,1)} %refs_1_.1) | copy-start | bytes 393220
  3.6 0.8 %copy-start.3 = (bf16[128,256]{1,0:T(8,128)(2,1)S(1)}, bf16[128,256]{1,0:T(8,128)(2,1)}, u32[]{:S(2)}) copy-start(bf16[128,256]{1,0:T(8,128)(2,1)} %refs_2_.1) | copy-start | bytes 196612
  4.5 0.7 %copy-start.4 = (s32[1,2,12]{2,1,0:T(2,128)S(1)}, s32[1,2,12]{2,1,0:T(2,128)}, u32[]{:S(2)}) copy-start(s32[1,2,12]{2,1,0:T(2,128)} %refs_4_.1) | copy-start | bytes 292
  5.1 0.7 %copy-start.5 = (s32[1,2,12]{2,1,0:T(2,128)S(1)}, s32[1,2,12]{2,1,0:T(2,128)}, u32[]{:S(2)}) copy-start(s32[1,2,12]{2,1,0:T(2,128)} %refs_5_.1) | copy-start | bytes 292
  5.8 0.7 %copy-start.6 = (s32[1,2]{1,0:T(1,128)S(1)}, s32[1,2]{1,0:T(1,128)}, u32[]{:S(2)}) copy-start(s32[1,2]{1,0:T(1,128)} %refs_6_.1) | copy-start | bytes 28

commit v4 on v3

--- a/solution.py
+++ b/solution.py
@@ -34,9 +34,9 @@
     (weight, cot, tiles, trows, tcols, tcount) = refs[10:16]
     (fbuf, amat, amat_t, pbuf, rbuf, dzfull, agg_t, aggs) = refs[16:24]
     (gsend, gpair, gbuf, gslots, wpart, wslots, wcol) = refs[24:31]
-    (pfull, weight_t, gterm, l_sem) = refs[31:35]
-    (f_send, f_recv, h_send, h_recv, p_send, p_recv, z_send, z_recv, a_send, a_recv) = refs[35:45]
-    (o_send, o_recv, g_send, g_recv, w_send, w_recv, c_send, c_recv, r_send, r_recv) = refs[45:]
+    (pfull, weight_t, gterm, wmine, wall, l_sem) = refs[31:37]
+    (f_send, f_recv, h_send, h_recv, p_send, p_recv, z_send, z_recv, a_send, a_recv) = refs[37:47]
+    (o_send, o_recv, g_send, g_recv, w_send, w_recv, c_send, c_recv, r_send, r_recv) = refs[47:]
     b = lax.axis_index("blk")
     r = lax.axis_index("rep")
     odd = lax.rem(b, 2)
@@ -333,41 +333,50 @@
     def r_copy(d):
         at_row = pl.ds(pl.multiple_of(r * w_rows, w_rows), w_rows)
         return remote(
-            wcol, wgrad.at[at_row], r_send.at[d - 1], r_recv.at[d - 1], (b, lax.rem(r + d, replicas))
+            wmine, wall.at[at_row], r_send.at[d - 1], r_recv.at[d - 1], (b, lax.rem(r + d, replicas))
         )
 
     def r_arrival(d):
         source = lax.rem(r + replicas - d, replicas)
         at_row = pl.ds(pl.multiple_of(source * w_rows, w_rows), w_rows)
-        return remote(wcol, wgrad.at[at_row], r_send.at[d - 1], r_recv.at[d - 1], (b, source))
-
-    for t in range(pairs):
-        gsend[t] = grad_terms(2 * t + 1).astype(gsend.dtype).reshape(gsend.shape[1:])
-        for k in range(replicas):
-            odd_copy(t, k).start()
-    for t in range(pairs):
-        gterm[t] = grad_terms(2 * t).reshape(gterm.shape[1:])
-
-    if whole_weight:
-        wpart[...] = weight_rows()
-        repeat(blocks, lambda d: w_copy(d).start(), 1)
-    else:
-        wgrad[...] = weight_rows()
-
-    for t in range(pairs):
-        for k in range(replicas):
-            send_grad(t, k)
-
-    if whole_weight:
+        return remote(wmine, wall.at[at_row], r_send.at[d - 1], r_recv.at[d - 1], (b, source))
+
+    def weight_sum():
         repeat(blocks, lambda d: w_copy(d).wait_recv(), 1)
         chunk = wpart[chunk_of(b), :]
         for d in range(1, blocks):
             chunk = chunk + wslots[d - 1]
         wcol[chunk_of(b), :] = chunk
         repeat(blocks, lambda d: c_copy(d).start(), 1)
+
+    def weight_gather():
         repeat(blocks, lambda d: c_arrival(d).wait_recv(), 1)
+        wmine[...] = wcol[...].astype(wmine.dtype)
         repeat(replicas, lambda d: r_copy(d).start(), 1)
-        wgrad[pl.ds(pl.multiple_of(r * w_rows, w_rows), w_rows), :] = wcol[...]
+
+    odd_first = grad_terms(1).astype(gsend.dtype).reshape(gsend.shape[1:])
+    gsend[0] = odd_first
+    for k in range(replicas):
+        odd_copy(0, k).start()
+    if whole_weight:
+        wpart[...] = weight_rows()
+        repeat(blocks, lambda d: w_copy(d).start(), 1)
+    else:
+        wgrad[...] = weight_rows()
+    for t in range(1, pairs):
+        gsend[t] = grad_terms(2 * t + 1).astype(gsend.dtype).reshape(gsend.shape[1:])
+        for k in range(replicas):
+            odd_copy(t, k).start()
+    for t in range(pairs):
+        gterm[t] = grad_terms(2 * t).reshape(gterm.shape[1:])
+
+    for t in range(pairs):
+        for k in range(replicas):
+            send_grad(t, k)
+            if whole_weight and t == 0 and k == 0:
+                weight_sum()
+            if whole_weight and t == pairs - 1 and k == max(replicas - 2, 0):
+                weight_gather()
 
     def grad_arrival(j):
         copy = remote(
@@ -383,6 +392,12 @@
     for j in range(1, blocks // 2):
         summed = summed + gslots[j].astype(jnp.float32)
     fgrad[...] = summed.astype(jnp.bfloat16)
+
+    if whole_weight:
+        at_row = pl.ds(pl.multiple_of(r * w_rows, w_rows), w_rows)
+        wall[at_row, :] = wmine[...]
+        repeat(replicas, lambda d: r_arrival(d).wait_recv(), 1)
+        wgrad[...] = wall[...].astype(jnp.float32)
 
     for t in range(pairs):
         for c, h in pieces:
@@ -402,7 +417,6 @@
     if whole_weight:
         repeat(blocks, lambda d: w_copy(d).wait_send(), 1)
         repeat(blocks, lambda d: c_copy(d).wait_send(), 1)
-        repeat(replicas, lambda d: r_arrival(d).wait_recv(), 1)
         repeat(replicas, lambda d: r_copy(d).wait_send(), 1)
 
 
@@ -455,6 +469,8 @@
             pltpu.VMEM((rows_blk, TILE), f32),
             pltpu.VMEM(weight.shape, bf16),
             pltpu.VMEM((pairs, replicas, own_rows, width), f32),
+            pltpu.VMEM((w_rows, width), bf16),
+            pltpu.VMEM((width, width), bf16),
             dma((6,)),
             dma((pairs, parts, HALVES)),
             dma((pairs, parts, HALVES)),
@@ -478,7 +494,7 @@
             dma((others,)),
         ],
         compiler_params=pltpu.CompilerParams(
-            collective_id=0, has_side_effects=True, vmem_limit_bytes=48 * 1024 * 1024
+            collective_id=0, has_side_effects=True
         ),
         name="graph_layer",
     )(features, weight, cotangent, tile_values, tile_rows, tile_cols, tile_count)

time: 56.9 us -> 49.8 us (0.88)
  local copies, waits for them, and re-layouts: 7.79 us -> 3.81 us
  Pallas kernels: 47.9 us -> 45.1 us
    unnamed x17 -> x5, local copies, waits for them, and re-layouts: 7.79 us -> 3.81 us
    pallas_call x1, Pallas kernels: 47.9 us -> 45.1 us  [per_device(): pl.pallas_call(functools.partial(kernel, dims), out_shape=(jax.ShapeDtype...]
where the time goes in v4:
time: 49.8 us; the launch traced here: 49.6 us
  Pallas kernels  45.1 us (91%)
  local copies, waits for them, and re-layouts  3.81 us (8%)
  between operations  0.64 us (1%)
    pallas_call x1, Pallas kernels, per_device(): pl.pallas_call(functools.partial(kernel, dims), out_shape=(jax.ShapeDtype...  45.1 us
    unnamed x5, local copies, waits for them, and re-layouts  3.81 us

profile of v4, /device:TPU:0, one launch (start us, length us, event | category | flops | bytes accessed | tf_op | source)
XLA Modules:
  0.0 49.6 jit_solution(18257496011276521102)
XLA Ops:
  0.6 45.1 %graph_layer.1 = (bf16[128,256]{1,0:T(8,128)(2,1)}, f32[256,256]{1,0:T(8,128)}, bf16[128,256]{1,0:T(8,128)(2,1)}) custom-call(bf16[512,256]{1,0:T(8,128)(2,1)} %refs_0_.1, bf16[256,256]{1,0:T(8,128)(2,1)} %refs_1_.1, bf16[128,256]{1,0:T(8,128)(2,1)} %refs_2_.1, bf16[1,2,12,128,128]{4,3,2,1,0:T(8,128)(2,1)} %refs_3_.1, s32[1,2,12]{2,1,0:T(2,128)} %refs_4_.1, ...), custom_call_target="tpu_custom_call" | custom-call | tf_op jit(solution)/shard_map/graph_layer/pallas_call | solution.py:438
  45.8 1.5 %copy.13 = bf16[128,256]{1,0:T(8,128)(2,1)} copy(bf16[128,256]{1,0:T(8,128)(2,1)} %get-tuple-element.6) | data formatting | bytes 131072
  47.2 0.0 copy-start
  47.2 1.7 %copy.14 = f32[256,256]{1,0:T(8,128)} copy(f32[256,256]{1,0:T(8,128)} %get-tuple-element.7) | data formatting | bytes 524288
  48.9 0.0 copy-done
  48.9 0.6 %copy.15 = bf16[128,256]{1,0:T(8,128)(2,1)} copy(bf16[128,256]{1,0:T(8,128)(2,1)S(1)} %copy-done) | data formatting | bytes 131072
Async XLA Ops:
  47.2 1.7 %copy-start = (bf16[128,256]{1,0:T(8,128)(2,1)S(1)}, bf16[128,256]{1,0:T(8,128)(2,1)}, u32[]{:S(2)}) copy-start(bf16[128,256]{1,0:T(8,128)(2,1)} %get-tuple-element.8) | copy-start | bytes 196612

commit v5 on v4

--- a/solution.py
+++ b/solution.py
@@ -34,9 +34,10 @@
     (weight, cot, tiles, trows, tcols, tcount) = refs[10:16]
     (fbuf, amat, amat_t, pbuf, rbuf, dzfull, agg_t, aggs) = refs[16:24]
     (gsend, gpair, gbuf, gslots, wpart, wslots, wcol) = refs[24:31]
-    (pfull, weight_t, gterm, wmine, wall, l_sem) = refs[31:37]
-    (f_send, f_recv, h_send, h_recv, p_send, p_recv, z_send, z_recv, a_send, a_recv) = refs[37:47]
-    (o_send, o_recv, g_send, g_recv, w_send, w_recv, c_send, c_recv, r_send, r_recv) = refs[47:]
+    (pfull, weight_t, gterm, wmine, wall, xbuf) = refs[31:37]
+    (x_send, x_recv, v_send, l_sem) = refs[37:41]
+    (f_send, f_recv, h_send, h_recv, p_send, p_recv, z_send, z_recv, a_send, a_recv) = refs[41:51]
+    (o_send, o_recv, g_send, g_recv, w_send, w_recv, c_send, c_recv, r_send, r_recv) = refs[51:]
     b = lax.axis_index("blk")
     r = lax.axis_index("rep")
     odd = lax.rem(b, 2)
@@ -44,6 +45,7 @@
     row_tiles = rows_blk // TILE
     column_parts = width // TILE
     whole_weight = w_chunk > 0
+    detour = replicas == 4 and sections == 2
     pieces = [(c, h) for c in range(column_parts) for h in range(HALVES)]
 
     def blk_at(offset):
@@ -124,11 +126,35 @@
         here = piece(2 * t + 1, c, h)
         return remote(here, here, h_send.at[t, c, h], h_recv.at[t, c, h], (neighbour, r))
 
+    def detour_copy(c):
+        return remote(
+            feature_piece(c, HALVES - 1),
+            xbuf.at[c],
+            x_send.at[c],
+            x_recv.at[c],
+            (blk_at(-2 * sections), 0),
+        )
+
+    def detour_hand(c):
+        return remote(
+            xbuf.at[c], piece(0, c, HALVES - 1), v_send.at[c], f_recv.at[0, c, HALVES - 1], (b, 2)
+        )
+
+    if detour:
+
+        @pl.when(r == 0)
+        def _():
+            for c in range(column_parts):
+                detour_copy(c).start()
+
+    def detoured(t, h):
+        return detour and t == 0 and h == HALVES - 1
+
     for c, h in pieces:
         for t in range(pairs):
             if t == 0:
 
-                @pl.when(r != 0)
+                @pl.when(jnp.logical_and(r != 0, r != 2) if detoured(t, h) else r != 0)
                 def _():
                     feature_copy(0, c, h).start()
 
@@ -170,9 +196,13 @@
         for t in range(pairs):
             if t == 0:
 
+                @pl.when(jnp.logical_and(r != 0, r != 2) if detoured(t, h) else r != 0)
+                def _():
+                    feature_copy(0, c, h).wait_send()
+
                 @pl.when(r != 0)
                 def _():
-                    feature_copy(0, c, h).wait()
+                    feature_copy(0, c, h).wait_recv()
 
                 @pl.when(r == 0)
                 def _():
@@ -183,6 +213,14 @@
         if n == 0:
             for s in range(pairs, sections):
                 place_tiles(s)
+
+    if detour:
+
+        @pl.when(r == 0)
+        def _():
+            for c in range(column_parts):
+                detour_copy(c).wait_recv()
+                detour_hand(c).start()
 
     def rows_of(k):
         return pl.ds(pl.multiple_of(k * own_rows, own_rows), own_rows)
@@ -399,6 +437,14 @@
         repeat(replicas, lambda d: r_arrival(d).wait_recv(), 1)
         wgrad[...] = wall[...].astype(jnp.float32)
 
+    if detour:
+
+        @pl.when(r == 0)
+        def _():
+            for c in range(column_parts):
+                detour_copy(c).wait_send()
+                detour_hand(c).wait_send()
+
     for t in range(pairs):
         for c, h in pieces:
             hand_copy(t, c, h).wait_send()
@@ -418,6 +464,14 @@
         repeat(blocks, lambda d: w_copy(d).wait_send(), 1)
         repeat(blocks, lambda d: c_copy(d).wait_send(), 1)
         repeat(replicas, lambda d: r_copy(d).wait_send(), 1)
+
+
+def publish(*refs):
+    copies = [pltpu.make_async_copy(refs[n], refs[3 + n], refs[6].at[n]) for n in range(3)]
+    for copy in copies:
+        copy.start()
+    for copy in copies:
+        copy.wait()
 
 
 def per_device(features, weight, cotangent, tile_values, tile_rows, tile_cols, tile_count):
@@ -471,6 +525,10 @@
             pltpu.VMEM((pairs, replicas, own_rows, width), f32),
             pltpu.VMEM((w_rows, width), bf16),
             pltpu.VMEM((width, width), bf16),
+            pltpu.VMEM((parts, rows_blk // HALVES, TILE), bf16),
+            dma((parts,)),
+            dma((parts,)),
+            dma((parts,)),
             dma((6,)),
             dma((pairs, parts, HALVES)),
             dma((pairs, parts, HALVES)),
@@ -500,7 +558,15 @@
     )(features, weight, cotangent, tile_values, tile_rows, tile_cols, tile_count)
     if not w_chunk:
         wgrad = lax.all_gather(lax.psum(wgrad, "blk"), "rep", axis=0, tiled=True)
-    return (act, wgrad, fgrad)
+    results = (act, wgrad, fgrad)
+    return pl.pallas_call(
+        publish,
+        out_shape=tuple(jax.ShapeDtypeStruct(x.shape, x.dtype) for x in results),
+        in_specs=[pl.BlockSpec(memory_space=pl.ANY)] * 3,
+        out_specs=(pl.BlockSpec(memory_space=pl.ANY),) * 3,
+        scratch_shapes=[dma((3,))],
+        name="publish",
+    )(*results)
 
 
 def solution(mesh):

time: 49.8 us -> 60 us (1.20)
  Pallas kernels: 45.1 us -> 59.2 us
  local copies, waits for them, and re-layouts: 3.81 us -> 0 us
    pallas_call x0 -> x1, Pallas kernels: none -> 13 us  [per_device(): pl.pallas_call(publish, out_shape=tuple((jax.ShapeDtypeStruct(x.shape, x....]
    unnamed x5 -> x0, local copies, waits for them, and re-layouts: 3.81 us -> none
    pallas_call x1, Pallas kernels: 45.1 us -> 46.2 us  [per_device(): pl.pallas_call(functools.partial(kernel, dims), out_shape=(jax.ShapeDtype...]
where the time goes in v5:
time: 60 us; the launch traced here: 59.9 us
  Pallas kernels  59.2 us (99%)
  between operations  0.64 us (1%)
    pallas_call x1, Pallas kernels, per_device(): pl.pallas_call(functools.partial(kernel, dims), out_shape=(jax.ShapeDtype...  46.2 us
    pallas_call x1, Pallas kernels, per_device(): pl.pallas_call(publish, out_shape=tuple((jax.ShapeDtypeStruct(x.shape, x....  13 us

profile of v5, /device:TPU:0, one launch (start us, length us, event | category | flops | bytes accessed | tf_op | source)
XLA Modules:
  0.0 59.9 jit_solution(5785834193448215269)
XLA Ops:
  0.6 46.2 %graph_layer.1 = (bf16[128,256]{1,0:T(8,128)(2,1)}, f32[256,256]{1,0:T(8,128)}, bf16[128,256]{1,0:T(8,128)(2,1)}) custom-call(bf16[512,256]{1,0:T(8,128)(2,1)} %refs_0_.1, bf16[256,256]{1,0:T(8,128)(2,1)} %refs_1_.1, bf16[128,256]{1,0:T(8,128)(2,1)} %refs_2_.1, bf16[1,2,12,128,128]{4,3,2,1,0:T(8,128)(2,1)} %refs_3_.1, s32[1,2,12]{2,1,0:T(2,128)} %refs_4_.1, ...), custom_call_target="tpu_custom_call" | custom-call | tf_op jit(solution)/shard_map/graph_layer/pallas_call | solution.py:492
  46.8 13.0 %publish.1 = (bf16[128,256]{1,0:T(8,128)(2,1)}, f32[256,256]{1,0:T(8,128)}, bf16[128,256]{1,0:T(8,128)(2,1)}) custom-call(bf16[128,256]{1,0:T(8,128)(2,1)} %get-tuple-element.6.refs_0_, f32[256,256]{1,0:T(8,128)} %get-tuple-element.7.refs_1_, bf16[128,256]{1,0:T(8,128)(2,1)} %get-tuple-element.8.refs_2_), custom_call_target="tpu_custom_call" | custom-call | tf_op jit(solution)/shard_map/publish/pallas_call | solution.py:562

commit v6 on v4

--- a/solution.py
+++ b/solution.py
@@ -34,9 +34,10 @@
     (weight, cot, tiles, trows, tcols, tcount) = refs[10:16]
     (fbuf, amat, amat_t, pbuf, rbuf, dzfull, agg_t, aggs) = refs[16:24]
     (gsend, gpair, gbuf, gslots, wpart, wslots, wcol) = refs[24:31]
-    (pfull, weight_t, gterm, wmine, wall, l_sem) = refs[31:37]
-    (f_send, f_recv, h_send, h_recv, p_send, p_recv, z_send, z_recv, a_send, a_recv) = refs[37:47]
-    (o_send, o_recv, g_send, g_recv, w_send, w_recv, c_send, c_recv, r_send, r_recv) = refs[47:]
+    (pfull, weight_t, gterm, wmine, wall, fown) = refs[31:37]
+    (s_sem, l_sem) = refs[37:39]
+    (f_send, f_recv, h_send, h_recv, p_send, p_recv, z_send, z_recv, a_send, a_recv) = refs[39:49]
+    (o_send, o_recv, g_send, g_recv, w_send, w_recv, c_send, c_recv, r_send, r_recv) = refs[49:]
     b = lax.axis_index("blk")
     r = lax.axis_index("rep")
     odd = lax.rem(b, 2)
@@ -67,7 +68,11 @@
             )
         )
     ]
-    for copy in local:
+    loads = [
+        pltpu.make_async_copy(feat.at[:, pl.ds(c * TILE, TILE)], fown.at[c], s_sem.at[c])
+        for c in range(column_parts)
+    ]
+    for copy in loads + local:
         copy.start()
 
     barrier = pltpu.get_barrier_semaphore()
@@ -95,7 +100,7 @@
         return fbuf.at[section, c, pl.ds(h * half_rows, half_rows)]
 
     def feature_piece(c, h):
-        return feat.at[pl.ds(h * half_rows, half_rows), pl.ds(c * TILE, TILE)]
+        return fown.at[c, pl.ds(h * half_rows, half_rows)]
 
     def feature_copy(t, c, h):
         return remote(
@@ -125,6 +130,8 @@
         return remote(here, here, h_send.at[t, c, h], h_recv.at[t, c, h], (neighbour, r))
 
     for c, h in pieces:
+        if h == 0:
+            loads[c].wait()
         for t in range(pairs):
             if t == 0:
 
@@ -418,6 +425,11 @@
         repeat(blocks, lambda d: w_copy(d).wait_send(), 1)
         repeat(blocks, lambda d: c_copy(d).wait_send(), 1)
         repeat(replicas, lambda d: r_copy(d).wait_send(), 1)
+
+
+def publish(*refs):
+    for n in range(3):
+        refs[3 + n][...] = refs[n][...]
 
 
 def per_device(features, weight, cotangent, tile_values, tile_rows, tile_cols, tile_count):
@@ -471,6 +483,8 @@
             pltpu.VMEM((pairs, replicas, own_rows, width), f32),
             pltpu.VMEM((w_rows, width), bf16),
             pltpu.VMEM((width, width), bf16),
+            pltpu.VMEM((parts, rows_blk, TILE), bf16),
+            dma((parts,)),
             dma((6,)),
             dma((pairs, parts, HALVES)),
             dma((pairs, parts, HALVES)),
@@ -500,7 +514,14 @@
     )(features, weight, cotangent, tile_values, tile_rows, tile_cols, tile_count)
     if not w_chunk:
         wgrad = lax.all_gather(lax.psum(wgrad, "blk"), "rep", axis=0, tiled=True)
-    return (act, wgrad, fgrad)
+    results = (act, wgrad, fgrad)
+    return pl.pallas_call(
+        publish,
+        out_shape=tuple(jax.ShapeDtypeStruct(x.shape, x.dtype) for x in results),
+        in_specs=[vmem] * 3,
+        out_specs=(vmem,) * 3,
+        name="publish",
+    )(*results)
 
 
 def solution(mesh):

time: 49.8 us -> 47.4 us (0.952)
  local copies, waits for them, and re-layouts: 3.81 us -> 0 us
  Pallas kernels: 45.1 us -> 46.6 us
    unnamed x5 -> x0, local copies, waits for them, and re-layouts: 3.81 us -> none
    pallas_call x0 -> x1, Pallas kernels: none -> 1.71 us  [per_device(): pl.pallas_call(publish, out_shape=tuple((jax.ShapeDtypeStruct(x.shape, x....]
where the time goes in v6:
time: 47.4 us; the launch traced here: 47.3 us
  Pallas kernels  46.6 us (98%)
  between operations  0.64 us (1%)
    pallas_call x1, Pallas kernels, per_device(): pl.pallas_call(functools.partial(kernel, dims), out_shape=(jax.ShapeDtype...  44.9 us
    pallas_call x1, Pallas kernels, per_device(): pl.pallas_call(publish, out_shape=tuple((jax.ShapeDtypeStruct(x.shape, x....  1.71 us

profile of v6, /device:TPU:0, one launch (start us, length us, event | category | flops | bytes accessed | tf_op | source)
XLA Modules:
  0.0 47.3 jit_solution(6257040962401232837)
XLA Ops:
  0.6 44.9 %graph_layer.1 = (bf16[128,256]{1,0:T(8,128)(2,1)}, f32[256,256]{1,0:T(8,128)}, bf16[128,256]{1,0:T(8,128)(2,1)}) custom-call(bf16[512,256]{1,0:T(8,128)(2,1)} %refs_0_.1, bf16[256,256]{1,0:T(8,128)(2,1)} %refs_1_.1, bf16[128,256]{1,0:T(8,128)(2,1)} %refs_2_.1, bf16[1,2,12,128,128]{4,3,2,1,0:T(8,128)(2,1)} %refs_3_.1, s32[1,2,12]{2,1,0:T(2,128)} %refs_4_.1, ...), custom_call_target="tpu_custom_call" | custom-call | tf_op jit(solution)/shard_map/graph_layer/pallas_call | solution.py:450
  45.5 1.7 %publish.1 = (bf16[128,256]{1,0:T(8,128)(2,1)}, f32[256,256]{1,0:T(8,128)}, bf16[128,256]{1,0:T(8,128)(2,1)}) custom-call(bf16[128,256]{1,0:T(8,128)(2,1)} %get-tuple-element.6.refs_0_, f32[256,256]{1,0:T(8,128)} %get-tuple-element.7.refs_1_, bf16[128,256]{1,0:T(8,128)(2,1)} %get-tuple-element.8.refs_2_), custom_call_target="tpu_custom_call" | custom-call | tf_op jit(solution)/shard_map/publish/pallas_call | solution.py:518

commit v7 on v6

--- a/solution.py
+++ b/solution.py
@@ -190,6 +190,9 @@
         if n == 0:
             for s in range(pairs, sections):
                 place_tiles(s)
+        if n == 1:
+            for s in range(1, sections, 2):
+                turn_tiles(s)
 
     def rows_of(k):
         return pl.ds(pl.multiple_of(k * own_rows, own_rows), own_rows)
@@ -220,8 +223,9 @@
         repeat(replicas, lambda d: partial_copy(d, c).start(), 1)
         pfull[...] = product
         totals.append(pfull[rows_of(r), :])
-    for s in range(1, sections, 2):
-        turn_tiles(s)
+        if c == 0:
+            for s in range(0, sections, 2):
+                turn_tiles(s)
     for copy in local[4:]:
         copy.wait()
     weight_t[...] = weight[...].T
@@ -264,8 +268,6 @@
     repeat(replicas, lambda d: agg_copy(d).start(), 1)
     aggs[0] = agg_t[pl.ds(pl.multiple_of(r * w_rows, w_rows), w_rows), :]
     act[...] = (z_value * sigma).astype(jnp.bfloat16)
-    for s in range(0, sections, 2):
-        turn_tiles(s)
 
     repeat(replicas, lambda d: dz_arrival(d).wait_recv(), 1)
     dy = jnp.dot(dzfull[...], weight_t[...], preferred_element_type=jnp.float32).astype(jnp.bfloat16)
@@ -363,13 +365,16 @@
 
     odd_first = grad_terms(1).astype(gsend.dtype).reshape(gsend.shape[1:])
     gsend[0] = odd_first
-    for k in range(replicas):
+    early = replicas // 2
+    for k in range(early):
         odd_copy(0, k).start()
     if whole_weight:
         wpart[...] = weight_rows()
         repeat(blocks, lambda d: w_copy(d).start(), 1)
     else:
         wgrad[...] = weight_rows()
+    for k in range(early, replicas):
+        odd_copy(0, k).start()
     for t in range(1, pairs):
         gsend[t] = grad_terms(2 * t + 1).astype(gsend.dtype).reshape(gsend.shape[1:])
         for k in range(replicas):
@@ -380,10 +385,10 @@
     for t in range(pairs):
         for k in range(replicas):
             send_grad(t, k)
-            if whole_weight and t == 0 and k == 0:
+            if whole_weight and t == pairs - 1 and k == early - 1:
                 weight_sum()
-            if whole_weight and t == pairs - 1 and k == max(replicas - 2, 0):
-                weight_gather()
+    if whole_weight:
+        weight_gather()
 
     def grad_arrival(j):
         copy = remote(

time: 47.4 us -> 45.9 us (0.968)
  Pallas kernels: 46.6 us -> 45.1 us
    pallas_call x1, Pallas kernels: 44.9 us -> 43.4 us  [per_device(): pl.pallas_call(functools.partial(kernel, dims), out_shape=(jax.ShapeDtype...]
where the time goes in v7:
time: 45.9 us; the launch traced here: 45.8 us
  Pallas kernels  45.1 us (98%)
  between operations  0.64 us (1%)
    pallas_call x1, Pallas kernels, per_device(): pl.pallas_call(functools.partial(kernel, dims), out_shape=(jax.ShapeDtype...  43.4 us
    pallas_call x1, Pallas kernels, per_device(): pl.pallas_call(publish, out_shape=tuple((jax.ShapeDtypeStruct(x.shape, x....  1.71 us

profile of v7, /device:TPU:0, one launch (start us, length us, event | category | flops | bytes accessed | tf_op | source)
XLA Modules:
  0.0 45.8 jit_solution(14603319486518924563)
XLA Ops:
  0.6 43.4 %graph_layer.1 = (bf16[128,256]{1,0:T(8,128)(2,1)}, f32[256,256]{1,0:T(8,128)}, bf16[128,256]{1,0:T(8,128)(2,1)}) custom-call(bf16[512,256]{1,0:T(8,128)(2,1)} %refs_0_.1, bf16[256,256]{1,0:T(8,128)(2,1)} %refs_1_.1, bf16[128,256]{1,0:T(8,128)(2,1)} %refs_2_.1, bf16[1,2,12,128,128]{4,3,2,1,0:T(8,128)(2,1)} %refs_3_.1, s32[1,2,12]{2,1,0:T(2,128)} %refs_4_.1, ...), custom_call_target="tpu_custom_call" | custom-call | tf_op jit(solution)/shard_map/graph_layer/pallas_call | solution.py:455
  44.1 1.7 %publish.1 = (bf16[128,256]{1,0:T(8,128)(2,1)}, f32[256,256]{1,0:T(8,128)}, bf16[128,256]{1,0:T(8,128)(2,1)}) custom-call(bf16[128,256]{1,0:T(8,128)(2,1)} %get-tuple-element.6.refs_0_, f32[256,256]{1,0:T(8,128)} %get-tuple-element.7.refs_1_, bf16[128,256]{1,0:T(8,128)(2,1)} %get-tuple-element.8.refs_2_), custom_call_target="tpu_custom_call" | custom-call | tf_op jit(solution)/shard_map/publish/pallas_call | solution.py:523

commit v8 on v7

--- a/solution.py
+++ b/solution.py
@@ -301,17 +301,23 @@
         term = gterm[t, k]
         odd_arrival(t, k).wait_recv()
         gbuf[t, k] = (term + gpair[t, k].astype(jnp.float32)).astype(gbuf.dtype)
-        if t == 0 and k == 0:
-
-            @pl.when(r != 0)
+        if t == 0:
+
+            @pl.when(jnp.logical_or(r != 0, k != 0))
             def _():
                 grad_copy(t, k).start()
 
-            @pl.when(r == 0)
+            @pl.when(jnp.logical_and(r == 0, k == 0))
             def _():
                 gslots[0] = gbuf[0, 0]
         else:
             grad_copy(t, k).start()
+
+    half = replicas // 2
+
+    def row_order(step, rep):
+        first = step // 2 + half * (step % 2)
+        return lax.rem(first + half * lax.rem(rep, 2), replicas)
 
     def weight_rows():
         repeat(replicas, lambda d: agg_copy(d).wait_recv(), 1)
@@ -367,24 +373,24 @@
     gsend[0] = odd_first
     early = replicas // 2
     for k in range(early):
-        odd_copy(0, k).start()
+        odd_copy(0, row_order(k, r + (odd if pairs == 1 else 0))).start()
     if whole_weight:
         wpart[...] = weight_rows()
         repeat(blocks, lambda d: w_copy(d).start(), 1)
     else:
         wgrad[...] = weight_rows()
     for k in range(early, replicas):
-        odd_copy(0, k).start()
+        odd_copy(0, row_order(k, r + (odd if pairs == 1 else 0))).start()
     for t in range(1, pairs):
         gsend[t] = grad_terms(2 * t + 1).astype(gsend.dtype).reshape(gsend.shape[1:])
         for k in range(replicas):
-            odd_copy(t, k).start()
+            odd_copy(t, row_order(k, r + (odd if t == pairs - 1 else 0))).start()
     for t in range(pairs):
         gterm[t] = grad_terms(2 * t).reshape(gterm.shape[1:])
 
     for t in range(pairs):
         for k in range(replicas):
-            send_grad(t, k)
+            send_grad(t, row_order(k, r))
             if whole_weight and t == pairs - 1 and k == early - 1:
                 weight_sum()
     if whole_weight:

time: 45.9 us -> 46.2 us (level)
  no operation moved by 1% of the time
where the time goes in v8:
time: 46.2 us; the launch traced here: 46.1 us
  Pallas kernels  45.5 us (98%)
  between operations  0.64 us (1%)
    pallas_call x1, Pallas kernels, per_device(): pl.pallas_call(functools.partial(kernel, dims), out_shape=(jax.ShapeDtype...  43.7 us
    pallas_call x1, Pallas kernels, per_device(): pl.pallas_call(publish, out_shape=tuple((jax.ShapeDtypeStruct(x.shape, x....  1.71 us

profile of v8, /device:TPU:0, one launch (start us, length us, event | category | flops | bytes accessed | tf_op | source)
XLA Modules:
  0.0 46.1 jit_solution(5518244219488413971)
XLA Ops:
  0.6 43.7 %graph_layer.1 = (bf16[128,256]{1,0:T(8,128)(2,1)}, f32[256,256]{1,0:T(8,128)}, bf16[128,256]{1,0:T(8,128)(2,1)}) custom-call(bf16[512,256]{1,0:T(8,128)(2,1)} %refs_0_.1, bf16[256,256]{1,0:T(8,128)(2,1)} %refs_1_.1, bf16[128,256]{1,0:T(8,128)(2,1)} %refs_2_.1, bf16[1,2,12,128,128]{4,3,2,1,0:T(8,128)(2,1)} %refs_3_.1, s32[1,2,12]{2,1,0:T(2,128)} %refs_4_.1, ...), custom_call_target="tpu_custom_call" | custom-call | tf_op jit(solution)/shard_map/graph_layer/pallas_call | solution.py:461
  44.4 1.7 %publish.1 = (bf16[128,256]{1,0:T(8,128)(2,1)}, f32[256,256]{1,0:T(8,128)}, bf16[128,256]{1,0:T(8,128)(2,1)}) custom-call(bf16[128,256]{1,0:T(8,128)(2,1)} %get-tuple-element.6.refs_0_, f32[256,256]{1,0:T(8,128)} %get-tuple-element.7.refs_1_, bf16[128,256]{1,0:T(8,128)(2,1)} %get-tuple-element.8.refs_2_), custom_call_target="tpu_custom_call" | custom-call | tf_op jit(solution)/shard_map/publish/pallas_call | solution.py:529

commit v9 on v7

--- a/solution.py
+++ b/solution.py
@@ -11,7 +11,7 @@
 MESH = pl.DeviceIdType.MESH
 TILE = 128
 UNROLL = 8
-HALVES = 2
+HALVES = 4
 
 
 def repeat(count, body, first=0):
@@ -190,7 +190,7 @@
         if n == 0:
             for s in range(pairs, sections):
                 place_tiles(s)
-        if n == 1:
+        if n == HALVES - 1:
             for s in range(1, sections, 2):
                 turn_tiles(s)
 

time: 45.9 us -> 46 us (level)
  no operation moved by 1% of the time
where the time goes in v9:
time: 46 us; the launch traced here: 45.8 us
  Pallas kernels  45.2 us (98%)
  between operations  0.64 us (1%)
    pallas_call x1, Pallas kernels, per_device(): pl.pallas_call(functools.partial(kernel, dims), out_shape=(jax.ShapeDtype...  43.5 us
    pallas_call x1, Pallas kernels, per_device(): pl.pallas_call(publish, out_shape=tuple((jax.ShapeDtypeStruct(x.shape, x....  1.71 us

profile of v9, /device:TPU:0, one launch (start us, length us, event | category | flops | bytes accessed | tf_op | source)
XLA Modules:
  0.0 45.8 jit_solution(17751351695731878676)
XLA Ops:
  0.6 43.5 %graph_layer.1 = (bf16[128,256]{1,0:T(8,128)(2,1)}, f32[256,256]{1,0:T(8,128)}, bf16[128,256]{1,0:T(8,128)(2,1)}) custom-call(bf16[512,256]{1,0:T(8,128)(2,1)} %refs_0_.1, bf16[256,256]{1,0:T(8,128)(2,1)} %refs_1_.1, bf16[128,256]{1,0:T(8,128)(2,1)} %refs_2_.1, bf16[1,2,12,128,128]{4,3,2,1,0:T(8,128)(2,1)} %refs_3_.1, s32[1,2,12]{2,1,0:T(2,128)} %refs_4_.1, ...), custom_call_target="tpu_custom_call" | custom-call | tf_op jit(solution)/shard_map/graph_layer/pallas_call | solution.py:455
  44.1 1.7 %publish.1 = (bf16[128,256]{1,0:T(8,128)(2,1)}, f32[256,256]{1,0:T(8,128)}, bf16[128,256]{1,0:T(8,128)(2,1)}) custom-call(bf16[128,256]{1,0:T(8,128)(2,1)} %get-tuple-element.6.refs_0_, f32[256,256]{1,0:T(8,128)} %get-tuple-element.7.refs_1_, bf16[128,256]{1,0:T(8,128)(2,1)} %get-tuple-element.8.refs_2_), custom_call_target="tpu_custom_call" | custom-call | tf_op jit(solution)/shard_map/publish/pallas_call | solution.py:523
